TPU v7x, 128 devices: a whole 4x4x4 slice. The times are simulated.
128 devices in a mesh: row: 8 (over x_hi, y), col: 16 (over x_lo, z, core).
Axes of the slice: x: 4 (x_hi: 2, x_lo: 2; x = x_hi * 2 + x_lo), y: 4, z: 4, core: 2. Of those that a mesh axis runs over, the one named last changes fastest.
Arguments:
- atom_feat: bfloat16 [32768, 128], P(('row', 'col')), may hold values from -6 to 6
- atom_token: int32 [32768], P(('row', 'col')), may hold values from 0 to 2047, as said below
- atom_count: int32 [128], P(('row', 'col')), may hold values from 128 to 256
- window_start: int32 [1024], P(('row', 'col')), may hold values from -64 to 192, as said below
- w_atom_qkv: bfloat16 [128, 384], replicated, may hold values from -2 to 2
- w_atom_out: bfloat16 [128, 128], replicated, may hold values from -0.5 to 0.5
- w_atom_tok: bfloat16 [128, 768], replicated, may hold values from -0.5 to 0.5
- single: bfloat16 [2048, 768], P(('row', 'col')), may hold values from -6 to 6
- tok_gain: float32 [768], replicated, may hold values from 0.1 to 1.9
- w_tok: bfloat16 [768, 3072], replicated, may hold values from -3 to 3
- w_tok_out: bfloat16 [768, 768], replicated, may hold values from -0.21875 to 0.21875
- pair: bfloat16 [2048, 2048, 128], P('row', 'col'), may hold values from -6 to 6
- w_pair_in: bfloat16 [128, 512], replicated, may hold values from -0.5 to 0.5
- w_pair_out: bfloat16 [256, 128], replicated, may hold values from -0.375 to 0.375
- w_bias: bfloat16 [128, 16], replicated, may hold values from -1.5 to 1.5
- w_back: bfloat16 [768, 128], replicated, may hold values from -0.21875 to 0.21875
Outputs:
- token_out: bfloat16 [2048, 768], P(('row', 'col'))
- atom_out: bfloat16 [32768, 128], P(('row', 'col'))
- pair_out: bfloat16 [2048, 2048, 128], P('row', 'col')
Inputs may be any that keep to these rules, and one draw needn't show every extreme that they name: `atom_token`: block d of 256 slots holds only tokens d * 16 to d * 16 + 15; over its first atom_count[d] slots the values never fall and name every token of the block; the other slots name the block's last token. `window_start`: window b of a block starts between 32 b - 64 and 32 b - 32.
All inputs are finite; a program needn't handle non-finite values.
Results may differ from a plain program's by a relative error of at most 0.008.
The roundings to bfloat16 on the way count: a program that leaves them out, or rounds other values in their place, can miss the bound.
Values may be sent and summed in bfloat16 or wider, within the bound.
A program may use at most 128 MiB of HBM per device.

v0:
```python
from functools import partial
import math

import jax
import jax.numpy as jnp
from jax import lax
from jax.sharding import PartitionSpec as P

ATOM_HEADS = 4
TOK_HEADS = 16
QUERY_BLOCK = 32
KEY_WINDOW = 128


eps = 1e-05


def shifted(block, axis, distance):
    devices = range(lax.axis_size(axis))
    route = [(i - distance, i) for i in devices if i - distance in devices]
    return lax.ppermute(block, axis, route)


def layer_norm(values):
    average = jnp.mean(values, axis=-1, keepdims=True)
    centred = values - average
    spread = jnp.mean(centred * centred, axis=-1, keepdims=True)
    return centred * lax.rsqrt(spread + eps)


def window_attention(queries, keys_values, present, starts):
    capacity, feat_width = queries.shape
    blocks = capacity // QUERY_BLOCK
    head_dim = feat_width // ATOM_HEADS

    def cut_window(offset):
        return (
            lax.dynamic_slice_in_dim(keys_values, offset, KEY_WINDOW, 0),
            lax.dynamic_slice_in_dim(present, offset, KEY_WINDOW, 0),
        )

    windows, allowed = jax.vmap(cut_window)(starts)
    key_rows = windows[:, :, :feat_width].reshape(blocks, KEY_WINDOW, ATOM_HEADS, head_dim)
    value_rows = windows[:, :, feat_width:].reshape(blocks, KEY_WINDOW, ATOM_HEADS, head_dim)
    grouped = queries.reshape(blocks, QUERY_BLOCK, ATOM_HEADS, head_dim)
    scores = jnp.einsum(
        "bqhd,bkhd->bhqk", grouped, key_rows, preferred_element_type=jnp.float32
    ) / math.sqrt(head_dim)
    scores = jnp.where(allowed[:, None, None, :], scores, -1e30)
    row_max = jnp.max(scores, axis=-1, keepdims=True)
    weights = jnp.exp(scores - row_max)
    weight_sum = jnp.sum(weights, axis=-1)
    blended = jnp.einsum(
        "bhqk,bkhd->bqhd",
        weights.astype(jnp.bfloat16),
        value_rows,
        preferred_element_type=jnp.float32,
    )
    blended = blended / jnp.transpose(weight_sum, (0, 2, 1))[:, :, :, None]
    return blended.reshape(capacity, feat_width).astype(jnp.bfloat16)


def one_block(
    features,
    prev_tail,
    next_head,
    live_count,
    starts,
    block_index,
    blocks_total,
    w_atom_qkv,
    w_atom_out,
):
    capacity, feat_width = features.shape
    halo_before = prev_tail.shape[0]
    halo_after = next_head.shape[0]
    ext_length = halo_before + capacity + halo_after
    extended = jnp.zeros((ext_length, feat_width), features.dtype)
    extended = lax.dynamic_update_slice_in_dim(extended, prev_tail, 0, 0)
    extended = lax.dynamic_update_slice_in_dim(extended, features, halo_before, 0)
    extended = lax.dynamic_update_slice_in_dim(extended, next_head, halo_before + live_count, 0)
    positions = jnp.arange(ext_length, dtype=jnp.int32)
    present = ((positions >= halo_before) | (block_index > 0)) & (
        (positions < halo_before + live_count)
        | (positions < halo_before + live_count + halo_after) & (block_index < blocks_total - 1)
    )
    queries = jnp.dot(
        features, w_atom_qkv[:, :feat_width], preferred_element_type=jnp.float32
    ).astype(jnp.bfloat16)
    keys_values = jnp.dot(
        extended, w_atom_qkv[:, feat_width:], preferred_element_type=jnp.float32
    ).astype(jnp.bfloat16)
    blended = window_attention(queries, keys_values, present, starts + halo_before)
    return (
        features.astype(jnp.float32)
        + jnp.dot(blended, w_atom_out, preferred_element_type=jnp.float32)
    ).astype(jnp.bfloat16)


def pair_piece(pair_tile, w_pair_in, w_pair_out, w_bias):
    tile_rows, tile_cols, channels = pair_tile.shape
    flat_tile = pair_tile.reshape(tile_rows * tile_cols, channels)
    normed = layer_norm(flat_tile.astype(jnp.float32)).astype(jnp.bfloat16)
    gate_up = jnp.dot(normed, w_pair_in, preferred_element_type=jnp.float32)
    hidden_width = w_pair_out.shape[0]
    hidden = (jax.nn.silu(gate_up[:, :hidden_width]) * gate_up[:, hidden_width:]).astype(
        jnp.bfloat16
    )
    updated = (
        flat_tile.astype(jnp.float32)
        + jnp.dot(hidden, w_pair_out, preferred_element_type=jnp.float32)
    ).astype(jnp.bfloat16)
    renormed = layer_norm(updated.astype(jnp.float32)).astype(jnp.bfloat16)
    pair_bias = jnp.einsum(
        "kh,pk->hp", w_bias, renormed, preferred_element_type=jnp.float32
    ).astype(jnp.bfloat16)
    return (
        updated.reshape(tile_rows, tile_cols, channels),
        pair_bias.reshape(-1, tile_rows, tile_cols),
    )


def attend(queries, keys_values, pair_bias):
    rows_here, feat_width = queries.shape
    head_dim = feat_width // TOK_HEADS
    query_rows = queries.reshape(rows_here, TOK_HEADS, head_dim)
    key_rows = keys_values[:, :feat_width].reshape(-1, TOK_HEADS, head_dim)
    value_rows = keys_values[:, feat_width:].reshape(-1, TOK_HEADS, head_dim)
    scores = jnp.einsum(
        "ihd,jhd->hij", query_rows, key_rows, preferred_element_type=jnp.float32
    ) / math.sqrt(head_dim)
    scores = scores + pair_bias.astype(jnp.float32)
    row_max = jnp.max(scores, axis=-1, keepdims=True)
    weights = jnp.exp(scores - row_max)
    weight_sum = jnp.sum(weights, axis=-1)
    blended = jnp.einsum(
        "hij,jhd->ihd", weights.astype(jnp.bfloat16), value_rows, preferred_element_type=jnp.float32
    )
    return (blended / jnp.transpose(weight_sum)[:, :, None]).reshape(rows_here, feat_width)


def local(
    atom_feat,
    atom_token,
    atom_count,
    window_start,
    w_atom_qkv,
    w_atom_out,
    w_atom_tok,
    single,
    tok_gain,
    w_tok,
    w_tok_out,
    pair,
    w_pair_in,
    w_pair_out,
    w_bias,
    w_back,
):
    capacity, atom_width = atom_feat.shape
    tok_dev, tok_width = single.shape
    flat_index = lax.axis_index(("row", "col"))
    device_count = lax.axis_size(("row", "col"))
    live_count = atom_count[0]
    halo_before = KEY_WINDOW // 2
    halo_after = KEY_WINDOW - QUERY_BLOCK
    tail_rows = lax.dynamic_slice_in_dim(atom_feat, live_count - halo_before, halo_before, 0)
    prev_tail = shifted(tail_rows, ("row", "col"), 1)
    next_head = shifted(atom_feat[:halo_after], ("row", "col"), -1)
    atom_mid = one_block(
        atom_feat,
        prev_tail,
        next_head,
        live_count,
        window_start,
        flat_index,
        device_count,
        w_atom_qkv,
        w_atom_out,
    )
    slot_ids = jnp.arange(capacity, dtype=jnp.int32)
    live_slot = slot_ids < live_count
    local_token = atom_token - flat_index * tok_dev
    member = (local_token[None, :] == jnp.arange(tok_dev, dtype=jnp.int32)[:, None]) & live_slot[
        None, :
    ]
    member_mask = member.astype(jnp.bfloat16)
    members = jnp.sum(member.astype(jnp.float32), axis=1)
    lifted = jax.nn.relu(jnp.dot(atom_mid, w_atom_tok, preferred_element_type=jnp.float32)).astype(
        jnp.bfloat16
    )
    pooled = jnp.dot(member_mask, lifted, preferred_element_type=jnp.float32) / members[:, None]
    tok_state = single.astype(jnp.float32) + pooled
    normed_tok = (layer_norm(tok_state) * tok_gain).astype(jnp.bfloat16)
    projected = jnp.dot(normed_tok, w_tok, preferred_element_type=jnp.float32).astype(jnp.bfloat16)
    queries = projected[:, :tok_width]
    gate_cols = projected[:, 3 * tok_width :]
    keys_values = lax.all_gather(
        projected[:, tok_width : 3 * tok_width], ("row", "col"), axis=0, tiled=True
    )
    tile_rows, tile_cols, channels = pair.shape
    row_pieces = math.gcd(tile_rows, 8)
    stacked = pair.reshape(row_pieces, tile_rows // row_pieces, tile_cols, channels)
    per_piece = partial(pair_piece, w_pair_in=w_pair_in, w_pair_out=w_pair_out, w_bias=w_bias)
    updated, bias_parts = lax.map(per_piece, stacked)
    pair_out = updated.reshape(tile_rows, tile_cols, channels)
    pair_bias = jnp.moveaxis(bias_parts, 1, 0).reshape(TOK_HEADS, tile_rows, tile_cols)
    bias_rows = lax.all_to_all(pair_bias, "col", split_axis=1, concat_axis=2, tiled=True)
    token_mixed = attend(queries, keys_values, bias_rows)
    gated_mix = (token_mixed * jax.nn.sigmoid(gate_cols.astype(jnp.float32))).astype(jnp.bfloat16)
    token_out = (
        tok_state + jnp.dot(gated_mix, w_tok_out, preferred_element_type=jnp.float32)
    ).astype(jnp.bfloat16)
    chosen = jnp.dot(
        jnp.transpose(member_mask), token_out, preferred_element_type=jnp.float32
    ).astype(jnp.bfloat16)
    atom_out = jnp.where(
        live_slot[:, None],
        atom_mid.astype(jnp.float32) + jnp.dot(chosen, w_back, preferred_element_type=jnp.float32),
        0.0,
    ).astype(jnp.bfloat16)
    return (token_out, atom_out, pair_out)


def solution(mesh):
    return jax.shard_map(
        local,
        mesh=mesh,
        in_specs=(
            P(("row", "col"), None),
            P(("row", "col")),
            P(("row", "col")),
            P(("row", "col")),
            P(),
            P(),
            P(),
            P(("row", "col"), None),
            P(),
            P(),
            P(),
            P("row", "col", None),
            P(),
            P(),
            P(),
            P(),
        ),
        out_specs=(P(("row", "col"), None), P(("row", "col"), None), P("row", "col", None)),
        check_vma=False,
    )
```

profile of v0, /device:TPU:1, one launch (start us, length us, event | category | flops | bytes accessed | tf_op | source)
XLA Modules:
  0.0 291.7 jit_solution(8898185485498519142)
XLA Ops:
  8.7 4.9 %collective-permute-start = (bf16[64,128]{1,0:T(8,128)(2,1)S(1)}, bf16[64,128]{1,0:T(8,128)(2,1)S(1)}, u32[]{:S(2)}, u32[]{:S(2)}) collective-permute-start(bf16[64,128]{1,0:T(8,128)(2,1)S(1)} %constant_dynamic-slice_fusion.2), channel_id=1, source_target_pairs={{0,1},{1,2},{2,3},{3,4},{4,5},{5,6},{6,7},{7,8},{8,9},{9,10},{10,1... | collective-permute-start | bytes 49160 | tf_op jit(solution)/shard_map/ppermute | solution.py:21
  14.4 1.9 collective-permute-start.1
  17.0 10.7 %while.16 = (s32[]{:T(128)}, pred[416]{0:T(512)(128)(4,1)S(1)}, s32[8,1]{0,1:T(1,128)S(1)}, pred[8,128]{1,0:T(8,128)(4,1)S(1)}, s32[]{:T(128)}, /*index=5*/s32[]{:T(128)}) while((s32[]{:T(128)}, pred[416]{0:T(512)(128)(4,1)S(1)}, s32[8,1]{0,1:T(1,128)S(1)}, pred[8,128]{1,0:T(8,128)(4,1)S(1)}, s32[]{:T(128)}, /*index=5*/s32[]{:T(128)}) %tuple.58), condition=%wide.while_cond.1, body=%wide.while_body.1.sunk | while | flops 2 | bytes 601 | solution.py:39
  33.1 15.0 %while.15 = (s32[]{:T(128)}, bf16[416,256]{1,0:T(8,128)(2,1)S(1)}, s32[8,2]{0,1:T(2,128)S(1)}, bf16[8,128,256]{2,1,0:T(8,128)(2,1)}, s32[]{:T(128)}) while((s32[]{:T(128)}, bf16[416,256]{1,0:T(8,128)(2,1)S(1)}, s32[8,2]{0,1:T(2,128)S(1)}, bf16[8,128,256]{2,1,0:T(8,128)(2,1)}, s32[]{:T(128)}) %tuple.55), condition=%wide.while_cond, body=%wide.while_body.sunk | while | flops 2 | bytes 132185 | solution.py:38
  41.1 1.3 bitcast_dynamic-update-slice_fusion.2
  46.8 1.3 bitcast_dynamic-update-slice_fusion.2
  52.1 3.1 %convolution_convert_fusion.1 = bf16[16,3072]{1,0:T(8,128)(2,1)S(1)} fusion(bf16[768,3072]{1,0:T(8,128)(2,1)} %param.27, f32[16,768]{1,0:T(8,128)S(1)} %get-tuple-element.100, f32[768]{0:T(1024)S(1)} %copy-done.6, f32[16]{0:T(128)S(1)} %add_rsqrt_fusion.1, f32[16]{0:T(128)S(1)} %broadcast_multiply_fusion.2), kind=kOutput, calls=%fused_computation.33 | convolution fusion | flops 75595776 | bytes 4869248 | tf_op jit(solution)/shard_map/dot_general | solution.py:195
  56.0 114.9 %while.14 = (s32[]{:T(128)}, bf16[8,32,128,128]{3,2,1,0:T(8,128)(2,1)}, bf16[8,16,32,128]{3,2,0,1:T(8,128)(2,1)S(1)}, bf16[8,32,128,128]{3,2,1,0:T(8,128)(2,1)},...) while((s32[]{:T(128)}, ...), condition=%wide.region_10.11_spmd, body=%wide.region_5.10_spmd.sunk | while | flops 840507392 | bytes 33673832 | solution.py:205
  56.0 1.6 convert_reduce_fusion.5
  57.6 2.3 multiply_reduce_fusion.3
  59.9 2.3 fusion.107
  63.4 1.5 dynamic-slice_convert_fusion.2
  64.9 1.4 convert_reduce_fusion.6
  67.7 1.5 fusion.110
  70.3 1.6 convert_reduce_fusion.5
  71.9 2.3 multiply_reduce_fusion.3
  74.3 2.3 fusion.107
  77.8 1.5 dynamic-slice_convert_fusion.2
  79.3 1.4 convert_reduce_fusion.6
  82.0 1.5 fusion.110
  84.7 1.6 convert_reduce_fusion.5
  86.3 2.3 multiply_reduce_fusion.3
  88.6 2.3 fusion.107
  92.2 1.5 dynamic-slice_convert_fusion.2
  93.6 1.4 convert_reduce_fusion.6
  96.4 1.5 fusion.110
  99.0 1.6 convert_reduce_fusion.5
  100.6 2.3 multiply_reduce_fusion.3
  103.0 2.3 fusion.107
  106.5 1.5 dynamic-slice_convert_fusion.2
  108.0 1.4 convert_reduce_fusion.6
  110.8 1.5 fusion.110
  113.4 1.6 convert_reduce_fusion.5
  115.0 2.3 multiply_reduce_fusion.3
  117.3 2.3 fusion.107
  120.9 1.5 dynamic-slice_convert_fusion.2
  122.4 1.4 convert_reduce_fusion.6
  125.1 1.5 fusion.110
  127.7 1.6 convert_reduce_fusion.5
  129.3 2.3 multiply_reduce_fusion.3
  131.7 2.3 fusion.107
  135.2 1.5 dynamic-slice_convert_fusion.2
  136.7 1.4 convert_reduce_fusion.6
  139.5 1.5 fusion.110
  142.1 1.6 convert_reduce_fusion.5
  143.7 2.3 multiply_reduce_fusion.3
  146.1 2.3 fusion.107
  149.6 1.5 dynamic-slice_convert_fusion.2
  151.1 1.4 convert_reduce_fusion.6
  153.8 1.5 fusion.110
  156.5 1.6 convert_reduce_fusion.5
  158.1 2.3 multiply_reduce_fusion.3
  160.4 2.3 fusion.107
  164.0 1.5 dynamic-slice_convert_fusion.2
  165.4 1.4 convert_reduce_fusion.6
  168.2 1.5 fusion.110
  170.8 1.7 copy.56
  172.5 6.3 %all-to-all-start = ((bf16[16,256,128]{2,0,1:T(8,128)(2,1)}), bf16[16,256,128]{2,0,1:T(8,128)(2,1)S(1)}, u32[]{:S(2)}, u32[]{:S(2)}) async-start(bf16[16,256,128]{2,0,1:T(8,128)(2,1)} %copy.56), calls=%async_computation | async-start | bytes 2097152 | tf_op jit(solution)/shard_map/all_to_all | solution.py:208
  179.0 17.5 %all-to-all-done = bf16[16,256,128]{2,0,1:T(8,128)(2,1)S(1)} async-done(((bf16[16,256,128]{2,0,1:T(8,128)(2,1)}), bf16[16,256,128]{2,0,1:T(8,128)(2,1)S(1)}, u32[]{:S(2)}, u32[]{:S(2)}) %all-to-all-start) | async-done | bytes 1048608 | tf_op jit(solution)/shard_map/all_to_all | solution.py:208
  196.7 66.9 %all-gather.2.cloned.1.call-done = bf16[2048,1536]{1,0:T(8,128)(2,1)} async-done(((bf16[16,1536]{1,0:T(8,128)(2,1)}), bf16[2048,1536]{1,0:T(8,128)(2,1)}) %all-gather.2.cloned.1.call-update) | async-done | bytes 6291472 | tf_op jit(solution)/shard_map/all_gather | solution.py:198
  263.6 5.9 %fusion.66 = (bf16[2048,768]{1,0:T(8,128)(2,1)}, bf16[2048,768]{1,0:T(8,128)(2,1)}) fusion(bf16[2048,1536]{1,0:T(8,128)(2,1)} %all-gather.2.cloned.1.call-done), kind=kLoop, calls=%fused_computation.105 | loop fusion | bytes 12582912 | tf_op jit(solution)/shard_map/slice | solution.py:127
  269.6 4.8 %copy.53 = bf16[2048,768]{0,1:T(8,128)(2,1)} copy(bf16[2048,768]{1,0:T(8,128)(2,1)} %get-tuple-element.93) | data formatting | bytes 6291456 | tf_op jit(solution)/shard_map/slice | solution.py:127
  274.4 4.7 %copy.52 = bf16[2048,768]{0,1:T(8,128)(2,1)} copy(bf16[2048,768]{1,0:T(8,128)(2,1)} %get-tuple-element.94) | data formatting | bytes 6291456 | tf_op jit(solution)/shard_map/slice | solution.py:128
  279.1 2.7 fusion.70
  (201 shorter events, 67.9 us)
Async XLA Ops:
  7.2 276.3 %copy-start = (bf16[768,768]{1,0:T(8,128)(2,1)S(1)}, bf16[768,768]{1,0:T(8,128)(2,1)}, u32[]{:S(2)}) copy-start(bf16[768,768]{1,0:T(8,128)(2,1)} %param.28) | copy-start | bytes 3538948
  7.2 256.5 %all-gather.2.cloned.1.call-start = ((), (), s32[]{:S(2)}) async-start(), calls=%async_computation.1 | async-start | bytes 6340608 | tf_op jit(solution)/shard_map/all_gather | solution.py:198
  8.7 22.1 %collective-permute-start = (bf16[64,128]{1,0:T(8,128)(2,1)S(1)}, bf16[64,128]{1,0:T(8,128)(2,1)S(1)}, u32[]{:S(2)}, u32[]{:S(2)}) collective-permute-start(bf16[64,128]{1,0:T(8,128)(2,1)S(1)} %constant_dynamic-slice_fusion.2), channel_id=1, source_target_pairs={{0,1},{1,2},{2,3},{3,4},{4,5},{5,6},{6,7},{7,8},{8,9},{9,10},{10,1... | collective-permute-start | bytes 49160 | tf_op jit(solution)/shard_map/ppermute | solution.py:21
  14.4 17.3 %collective-permute-start.1 = (bf16[96,128]{1,0:T(8,128)(2,1)S(1)}, bf16[96,128]{1,0:T(8,128)(2,1)S(1)}, u32[]{:S(2)}, u32[]{:S(2)}) collective-permute-start(bf16[96,128]{1,0:T(8,128)(2,1)S(1)} %slice.36), channel_id=1, source_target_pairs={{1,0},{2,1},{3,2},{4,3},{5,4},{6,5},{7,6},{8,7},{9,8},{10,9},{11,1... | collective-permute-start | bytes 73736 | tf_op jit(solution)/shard_map/ppermute | solution.py:21
  28.7 3.0 %copy-start.10 = (pred[256]{0:T(512)(128)(4,1)}, pred[256]{0:T(512)(128)(4,1)S(1)}, u32[]{:S(2)}) copy-start(pred[256]{0:T(512)(128)(4,1)S(1)} %iota_compare_fusion.4) | copy-start | bytes 772
  29.4 0.6 copy-start.7
  49.9 1.2 copy-start.3
  49.9 1.2 copy-start.4
  49.9 1.4 copy-start.8
  49.9 1.4 copy-start.11
  49.9 1.4 copy-start.13
  49.9 1.4 copy-start.14
  50.0 1.4 copy-start.17
  50.4 1.7 copy-start.6
  52.1 3.8 %copy-start.2 = (bf16[128,512]{1,0:T(8,128)(2,1)S(1)}, bf16[128,512]{1,0:T(8,128)(2,1)}, u32[]{:S(2)}) copy-start(bf16[128,512]{1,0:T(8,128)(2,1)} %param.30) | copy-start | bytes 393220
  52.1 3.8 %copy-start.16 = (bf16[256,128]{1,0:T(8,128)(2,1)S(1)}, bf16[256,128]{1,0:T(8,128)(2,1)}, u32[]{:S(2)}) copy-start(bf16[256,128]{1,0:T(8,128)(2,1)} %param.31) | copy-start | bytes 196612
  52.1 3.8 %copy-start.18 = (bf16[128,16]{0,1:T(8,128)(2,1)S(1)}, bf16[128,16]{0,1:T(8,128)(2,1)}, u32[]{:S(2)}) copy-start(bf16[128,16]{0,1:T(8,128)(2,1)} %param.32) | copy-start | bytes 12292
  172.5 24.0 %all-to-all-start = ((bf16[16,256,128]{2,0,1:T(8,128)(2,1)}), bf16[16,256,128]{2,0,1:T(8,128)(2,1)S(1)}, u32[]{:S(2)}, u32[]{:S(2)}) async-start(bf16[16,256,128]{2,0,1:T(8,128)(2,1)} %copy.56), calls=%async_computation | async-start | bytes 2097152 | tf_op jit(solution)/shard_map/all_to_all | solution.py:208
  279.1 3.1 %copy-start.1 = (bf16[2048,768]{0,1:T(8,128)(2,1)S(1)}, bf16[2048,768]{0,1:T(8,128)(2,1)}, u32[]{:S(2)}) copy-start(bf16[2048,768]{0,1:T(8,128)(2,1)} %copy.52) | copy-start | bytes 9437188
  282.2 1.5 copy-start.9
  282.2 1.5 copy-start.12
  282.2 1.5 copy-start.15
  283.7 1.1 copy-start.5
Sparse Core Ops, SparseCore 0:
  56.0 207.5 all-gather.1
where the time goes:
time: 293 us; the launch traced here: 292 us
  waiting for transfers between devices  84.4 us (29%)
  other arithmetic  74.9 us (26%)
  local copies, waits for them, and re-layouts  58.4 us (20%)
  matrix products  44.8 us (15%)
  between operations  15.2 us (5%)
  starting transfers between devices  13.2 us (5%)
    all_gather x1, waiting for transfers between devices, local(): lax.all_gather(projected[:, tok_width:3 * tok_width], ('row', 'col'), axi...  66.9 us
    reduce_sum x17, other arithmetic, layer_norm(): spread = jnp.mean(centred * centred, axis=-1, keepdims=True)  29.1 us
    gather x48, local copies, waits for them, and re-layouts  25.7 us
    convert_element_type x8, other arithmetic, pair_piece(): normed = layer_norm(flat_tile.astype(jnp.float32)).astype(jnp.bfloat16)  18.4 us
    all_to_all x1, waiting for transfers between devices, local(): lax.all_to_all(pair_bias, 'col', split_axis=1, concat_axis=2, tiled=True)  17.5 us
    reduce_sum x8, other arithmetic, layer_norm(): average = jnp.mean(values, axis=-1, keepdims=True)  12.6 us
    convert_element_type x8, other arithmetic, pair_piece(): flat_tile.astype(jnp.float32)  11.8 us
    dot_general x8, matrix products, pair_piece(): jnp.einsum('kh,pk->hp', w_bias, renormed, preferred_element_type=jnp.floa...  11.7 us
  transfers between devices with their start and end apart: 4, of which 2 were waited for; matrix products, arithmetic and copies ran while one was open for 45% of the time, Pallas kernels for 0%

commit v1 on v0

v1 whole, which is shorter than its diff:
```python
import functools
import math

import jax
import jax.numpy as jnp
from jax import lax
from jax.experimental import pallas as pl
from jax.experimental.pallas import tpu as pltpu
from jax.sharding import PartitionSpec as P

ATOM_HEADS = 4
TOK_HEADS = 16
QUERY_BLOCK = 32
KEY_WINDOW = 128
BEFORE = KEY_WINDOW // 2
AFTER = KEY_WINDOW - QUERY_BLOCK
CAP = 256
TOK_DEV = 16
C_ATOM = 128
C_TOK = 768
C_PAIR = 128
HID = 256
ROWS = 8
COLS = 16
TILE_I = 256
TILE_J = 128
MESSAGE = C_TOK + 128
EPS = 1e-05

f32 = jnp.float32
bf16 = jnp.bfloat16
MESH = pl.DeviceIdType.MESH
VMEM = pl.BlockSpec(memory_space=pltpu.VMEM)
SMEM = pl.BlockSpec(memory_space=pltpu.SMEM)
ANY = pl.BlockSpec(memory_space=pl.ANY)


def dot(a, b):
    return jnp.dot(a, b, preferred_element_type=f32)


def dot_nt(a, b):
    return lax.dot_general(a, b, (((1,), (1,)), ((), ())), preferred_element_type=f32)


def iota(shape, dim):
    return lax.broadcasted_iota(jnp.int32, shape, dim)


def shifted(block, axis, distance):
    devices = range(lax.axis_size(axis))
    route = [(i - distance, i) for i in devices if i - distance in devices]
    return lax.ppermute(block, axis, route)


def membership(token, live_count, block):
    shape = (TOK_DEV, CAP)
    local = token - block * TOK_DEV
    return ((iota(shape, 0) == local) & (iota(shape, 1) < live_count)).astype(f32)


def atom_kernel(
    count_ref, starts_ref, feat_ref, tail_ref, head_ref, token_ref, w_qkv_ref, w_out_ref, w_lift_ref,
    single_ref, gain_ref, w_tok_ref, mid_ref, state_ref, query_ref, kv_ref, gate_ref,
):
    block = lax.axis_index("row") * COLS + lax.axis_index("col")
    last = ROWS * COLS - 1
    count = count_ref[0]
    feat = feat_ref[...]
    rows = jnp.concatenate([tail_ref[...], feat, head_ref[...]], axis=0)
    length = rows.shape[0]
    queries = dot(feat, w_qkv_ref[:, :C_ATOM]).astype(bf16)
    keys_values = dot(rows, w_qkv_ref[:, C_ATOM:]).astype(bf16)
    keys, values = keys_values[:, :C_ATOM], keys_values[:, C_ATOM:]
    index = iota((1, length), 1)
    absent = -(1 << 20)
    shift_tail = jnp.where(block > 0, 0, absent)
    shift_head = jnp.where(block < last, count - CAP, absent)
    shift_own = jnp.where(index < BEFORE + count, 0, absent)
    position = index + jnp.where(
        index < BEFORE, shift_tail, jnp.where(index < BEFORE + CAP, shift_own, shift_head)
    )
    window = iota((CAP, 1), 0) // QUERY_BLOCK
    start = jnp.zeros((CAP, 1), jnp.int32)
    for b in range(CAP // QUERY_BLOCK):
        start = jnp.where(window == b, starts_ref[b] + BEFORE, start)
    allowed = (position >= start) & (position < start + KEY_WINDOW)
    width = C_ATOM // ATOM_HEADS
    lane = iota((CAP, C_ATOM), 1)
    mixed = jnp.zeros((CAP, C_ATOM), f32)
    for h in range(ATOM_HEADS):
        mine = (lane >= h * width) & (lane < (h + 1) * width)
        scores = dot_nt(jnp.where(mine, queries, jnp.zeros_like(queries)), keys)
        scores = jnp.where(allowed, scores * (1.0 / math.sqrt(width)), -1e30)
        weights = jnp.exp(scores - jnp.max(scores, axis=1, keepdims=True))
        total = jnp.sum(weights, axis=1, keepdims=True)
        mixed = jnp.where(mine, dot(weights.astype(bf16), values) / total, mixed)
    mid = (feat.astype(f32) + dot(mixed.astype(bf16), w_out_ref[...])).astype(bf16)
    mid_ref[...] = mid
    lifted = jnp.maximum(dot(mid, w_lift_ref[...]), 0.0).astype(bf16)
    member = membership(token_ref[...], count, block)
    members = jnp.sum(member, axis=1, keepdims=True)
    state = single_ref[...].astype(f32) + dot(member.astype(bf16), lifted) / members
    state_ref[...] = state
    centred = state - jnp.mean(state, axis=1, keepdims=True)
    spread = jnp.mean(centred * centred, axis=1, keepdims=True)
    normed = (centred * lax.rsqrt(spread + EPS) * gain_ref[...]).astype(bf16)
    query_ref[...] = dot(normed, w_tok_ref[:, :C_TOK]).astype(bf16)
    kv_ref[...] = dot(normed, w_tok_ref[:, C_TOK : 3 * C_TOK]).astype(bf16)
    gate_ref[...] = dot(normed, w_tok_ref[:, 3 * C_TOK :]).astype(bf16)


def atom_part(count, starts, feat, tail, head, token, w_qkv, w_out, w_lift, single, gain, w_tok):
    return pl.pallas_call(
        atom_kernel,
        out_shape=[
            jax.ShapeDtypeStruct((CAP, C_ATOM), bf16),
            jax.ShapeDtypeStruct((TOK_DEV, C_TOK), f32),
            jax.ShapeDtypeStruct((TOK_DEV, C_TOK), bf16),
            jax.ShapeDtypeStruct((TOK_DEV, 2 * C_TOK), bf16),
            jax.ShapeDtypeStruct((TOK_DEV, C_TOK), bf16),
        ],
        in_specs=[SMEM, SMEM] + [VMEM] * 10,
        out_specs=[VMEM] * 5,
        compiler_params=pltpu.CompilerParams(vmem_limit_bytes=32 << 20),
        name="atom_part",
    )(count, starts, feat, tail, head, token, w_qkv, w_out, w_lift, single, gain, w_tok)


def exchange_kernel(query_ref, kv_ref, queries_ref, kvs_ref, q_send, q_recv, kv_send, kv_recv):
    r, c = lax.axis_index("row"), lax.axis_index("col")
    self_kv = c == 2 * r + c // 8
    barrier = pltpu.get_barrier_semaphore()

    def source(k):
        return c // 2, lax.rem(c, 2) * 8 + k

    for k in range(1, COLS):
        pl.semaphore_signal(
            barrier, inc=1, device_id=(r, lax.rem(c + k, COLS)), device_id_type=MESH
        )
    for k in range(ROWS):
        sr, sc = source(k)

        @pl.when((sr != r) | (sc != c))
        def _():
            pl.semaphore_signal(barrier, inc=1, device_id=(sr, sc), device_id_type=MESH)

    pl.semaphore_wait(barrier, COLS - 1 + ROWS - self_kv.astype(jnp.int32))

    def q_copy(k):
        return pltpu.make_async_remote_copy(
            src_ref=query_ref,
            dst_ref=queries_ref.at[c],
            send_sem=q_send.at[k],
            recv_sem=q_recv.at[c],
            device_id=(r, lax.rem(c + k, COLS)),
            device_id_type=MESH,
        )

    def q_arrival(k):
        s = lax.rem(c + k, COLS)
        return pltpu.make_async_remote_copy(
            src_ref=query_ref,
            dst_ref=queries_ref.at[s],
            send_sem=q_send.at[k],
            recv_sem=q_recv.at[s],
            device_id=(r, s),
            device_id_type=MESH,
        )

    def kv_copy(k):
        slot = lax.rem(c, 8)
        return pltpu.make_async_remote_copy(
            src_ref=kv_ref,
            dst_ref=kvs_ref.at[slot],
            send_sem=kv_send.at[k],
            recv_sem=kv_recv.at[slot],
            device_id=(k, 2 * r + c // 8),
            device_id_type=MESH,
        )

    def kv_arrival(k):
        sr, sc = source(k)
        return pltpu.make_async_remote_copy(
            src_ref=kv_ref,
            dst_ref=kvs_ref.at[k],
            send_sem=kv_send.at[k],
            recv_sem=kv_recv.at[k],
            device_id=(sr, sc),
            device_id_type=MESH,
        )

    def elsewhere(k):
        return (k != r) | (2 * r + c // 8 != c)

    for k in range(ROWS):

        @pl.when(elsewhere(k))
        def _():
            kv_copy(k).start()

    for k in range(1, COLS):
        q_copy(k).start()
    queries_ref[c] = query_ref[...]

    @pl.when(self_kv)
    def _():
        kvs_ref[lax.rem(c, 8)] = kv_ref[...]

    for k in range(ROWS):
        sr, sc = source(k)

        @pl.when((sr != r) | (sc != c))
        def _():
            kv_arrival(k).wait_recv()

        @pl.when(elsewhere(k))
        def _():
            kv_copy(k).wait_send()

    for k in range(1, COLS):
        q_arrival(k).wait_recv()
        q_copy(k).wait_send()


def exchange(query, kv):
    return pl.pallas_call(
        exchange_kernel,
        out_shape=[
            jax.ShapeDtypeStruct((COLS, TOK_DEV, C_TOK), bf16),
            jax.ShapeDtypeStruct((ROWS, TOK_DEV, 2 * C_TOK), bf16),
        ],
        in_specs=[VMEM] * 2,
        out_specs=[VMEM] * 2,
        scratch_shapes=[
            pltpu.SemaphoreType.DMA((COLS,)),
            pltpu.SemaphoreType.DMA((COLS,)),
            pltpu.SemaphoreType.DMA((ROWS,)),
            pltpu.SemaphoreType.DMA((ROWS,)),
        ],
        compiler_params=pltpu.CompilerParams(
            collective_id=0, has_side_effects=True, vmem_limit_bytes=16 << 20
        ),
        name="exchange",
    )(query, kv)


PAIR_ROWS = 32


def pair_kernel(
    pair_ref, w_in_ref, w_out_ref, w_bias_ref, out_ref, bias_ref, held, done, in_sem, out_sem, w_up, w_down
):
    pieces = TILE_I // PAIR_ROWS
    positions = PAIR_ROWS * TILE_J

    def rows(k):
        return pl.ds(k * PAIR_ROWS, PAIR_ROWS)

    def load(k):
        return pltpu.make_async_copy(pair_ref.at[rows(k)], held.at[rows(k)], in_sem.at[k])

    def store(k):
        return pltpu.make_async_copy(done.at[rows(k)], out_ref.at[rows(k)], out_sem.at[k])

    for k in range(pieces):
        load(k).start()
    w_in = w_in_ref[...].astype(f32)
    w_up[:HID] = (w_in[:, :HID].T * 0.5).astype(bf16)
    w_up[HID : 2 * HID] = w_in[:, HID:].T.astype(bf16)
    w_bias = w_bias_ref[...].astype(f32).T
    w_up[2 * HID :] = w_bias.astype(bf16)
    w_down[:C_PAIR] = w_out_ref[...].astype(f32).T.astype(bf16)
    w_down[C_PAIR:] = lax.dot_general(
        w_bias_ref[...], w_out_ref[...], (((0,), (1,)), ((), ())), preferred_element_type=f32
    ).astype(bf16)
    bias_sum = jnp.sum(w_bias, axis=1, keepdims=True)
    share = 1.0 / C_PAIR

    def step(k, carry):
        load(k).wait()
        tile = held[rows(k)].reshape(positions, C_PAIR).T
        wide = tile.astype(f32)
        mean = jnp.sum(wide, axis=0, keepdims=True) * share
        centred = wide - mean
        spread = jnp.sum(centred * centred, axis=0, keepdims=True) * share + EPS
        scale = lax.rsqrt(spread)
        up = dot(w_up[...], (centred * scale).astype(bf16))
        gate, value = up[:HID].astype(bf16), up[HID : 2 * HID].astype(bf16)
        hidden = (gate + gate * jnp.tanh(gate)) * value
        down = dot(w_down[...], hidden)
        updated = (wide + down[:C_PAIR]).astype(bf16)
        done[rows(k)] = updated.T.reshape(PAIR_ROWS, TILE_J, C_PAIR)
        store(k).start()
        again = updated.astype(f32)
        mean_again = jnp.sum(again, axis=0, keepdims=True) * share
        centred = again - mean_again
        spread_again = jnp.sum(centred * centred, axis=0, keepdims=True) * share + EPS
        bias = up[2 * HID :] * (spread * scale) + down[C_PAIR:] + bias_sum * (mean - mean_again)
        bias = (bias * lax.rsqrt(spread_again)).astype(bf16)
        for i in range(PAIR_ROWS):
            bias_ref[k * PAIR_ROWS + i] = bias[:, i * TILE_J : (i + 1) * TILE_J]
        return carry

    lax.fori_loop(0, pieces, step, 0)
    for k in range(pieces):
        store(k).wait()


def pair_part(pair, w_in, w_out, w_bias):
    pieces = TILE_I // PAIR_ROWS
    return pl.pallas_call(
        pair_kernel,
        out_shape=[
            jax.ShapeDtypeStruct(pair.shape, bf16),
            jax.ShapeDtypeStruct((TILE_I, TOK_HEADS, TILE_J), bf16),
        ],
        in_specs=[ANY, VMEM, VMEM, VMEM],
        out_specs=[ANY, VMEM],
        scratch_shapes=[
            pltpu.VMEM((TILE_I, TILE_J, C_PAIR), bf16),
            pltpu.VMEM((TILE_I, TILE_J, C_PAIR), bf16),
            pltpu.SemaphoreType.DMA((pieces,)),
            pltpu.SemaphoreType.DMA((pieces,)),
            pltpu.VMEM((2 * HID + TOK_HEADS, C_PAIR), bf16),
            pltpu.VMEM((C_PAIR + TOK_HEADS, HID), bf16),
        ],
        compiler_params=pltpu.CompilerParams(vmem_limit_bytes=48 << 20),
        name="pair_part",
    )(pair, w_in, w_out, w_bias)


def attend_kernel(
    count_ref, queries_ref, kvs_ref, bias_ref, gate_ref, state_ref, mid_ref, token_ref, w_tok_out_ref, w_back_ref,
    token_out_ref, atom_out_ref, outbox, inbox, send_sem, recv_sem,
):
    r, c = lax.axis_index("row"), lax.axis_index("col")
    block = r * COLS + c
    width = C_TOK // TOK_HEADS
    barrier = pltpu.get_barrier_semaphore()
    for k in range(1, COLS):
        pl.semaphore_signal(
            barrier, inc=1, device_id=(r, lax.rem(c + k, COLS)), device_id_type=MESH
        )
    pl.semaphore_wait(barrier, COLS - 1)

    def copy(k):
        to = lax.rem(c + k, COLS)
        return pltpu.make_async_remote_copy(
            src_ref=outbox.at[to],
            dst_ref=inbox.at[c],
            send_sem=send_sem.at[to],
            recv_sem=recv_sem.at[c],
            device_id=(r, to),
            device_id_type=MESH,
        )

    def arrival(k):
        s = lax.rem(c + k, COLS)
        return pltpu.make_async_remote_copy(
            src_ref=outbox.at[s],
            dst_ref=inbox.at[s],
            send_sem=send_sem.at[s],
            recv_sem=recv_sem.at[s],
            device_id=(r, s),
            device_id_type=MESH,
        )

    head = iota((TOK_HEADS, C_TOK), 0) * width
    column = iota((TOK_HEADS, C_TOK), 1)
    in_head = (column >= head) & (column < head + width)
    head_one = in_head.astype(bf16)
    head_one_wide = in_head.astype(f32)
    lane_pick = (iota((TOK_HEADS, 128), 0) == iota((TOK_HEADS, 128), 1)).astype(f32)
    kvs = kvs_ref[...].reshape(TILE_J, 2 * C_TOK)
    keys, values = kvs[:, :C_TOK], kvs[:, C_TOK:]

    def partial(to):
        spread = queries_ref[to][:, None, :] * head_one[None]
        scores = dot_nt(spread.reshape(TOK_DEV * TOK_HEADS, C_TOK), keys)
        bias = bias_ref[pl.ds(to * TOK_DEV, TOK_DEV)].reshape(TOK_DEV * TOK_HEADS, TILE_J)
        scores = scores * (1.0 / math.sqrt(width)) + bias.astype(f32)
        top = jnp.max(scores, axis=1, keepdims=True).astype(bf16).astype(f32)
        weights = jnp.exp(scores - top)
        total = jnp.sum(weights, axis=1, keepdims=True)
        mixed = dot(weights.astype(bf16), values).reshape(TOK_DEV, TOK_HEADS, C_TOK)
        mixed = jnp.sum(mixed * head_one_wide[None], axis=1)

        def to_lanes(column_values):
            wide = jnp.broadcast_to(column_values, (TOK_DEV * TOK_HEADS, 128))
            return jnp.sum(wide.reshape(TOK_DEV, TOK_HEADS, 128) * lane_pick[None], axis=1)

        tops = to_lanes(top)[:, :TOK_HEADS]
        totals = to_lanes(total)[:, :TOK_HEADS]
        high = totals.astype(bf16)
        low = (totals - high.astype(f32)).astype(bf16)
        return mixed.astype(bf16), tops.astype(bf16), high, low

    def put(box, at, parts):
        mixed, tops, high, low = parts
        rest = jnp.zeros((TOK_DEV, 128 - 3 * TOK_HEADS), bf16)
        box[at, :, :C_TOK] = mixed
        box[at, :, C_TOK:] = jnp.concatenate([tops, high, low, rest], axis=1)

    def one(k, carry):
        to = lax.rem(c + k, COLS)
        put(outbox, to, partial(to))
        copy(k).start()
        return carry

    lax.fori_loop(1, COLS, one, 0)
    put(inbox, c, partial(c))

    def arrived(k, carry):
        arrival(k).wait_recv()
        copy(k).wait_send()
        return carry

    lax.fori_loop(1, COLS, arrived, 0)
    n = TOK_HEADS
    tails = [inbox[s, :, C_TOK:].astype(f32) for s in range(COLS)]
    tops = [t[:, :n] for t in tails]
    totals = [t[:, n : 2 * n] + t[:, 2 * n : 3 * n] for t in tails]
    top = functools.reduce(jnp.maximum, tops)
    factors = [jnp.exp(t - top) for t in tops]
    total = sum(f * t for f, t in zip(factors, totals))
    factors = jnp.concatenate([f / total for f in factors], axis=0)
    high = factors.astype(bf16)
    low = (factors - high.astype(f32)).astype(bf16)
    factors = dot(high, head_one) + dot(low, head_one)
    mixed = sum(
        factors[s * TOK_DEV : (s + 1) * TOK_DEV] * inbox[s, :, :C_TOK].astype(f32)
        for s in range(COLS)
    )
    gated = (mixed * jax.nn.sigmoid(gate_ref[...].astype(f32))).astype(bf16)
    token_out = (state_ref[...] + dot(gated, w_tok_out_ref[...])).astype(bf16)
    token_out_ref[...] = token_out
    count = count_ref[0]
    member = membership(token_ref[...], count, block).astype(bf16)
    same = (iota((CAP, CAP), 0) == iota((CAP, CAP), 1)).astype(bf16)
    chosen = dot(dot_nt(same, member).astype(bf16), token_out).astype(bf16)
    back = mid_ref[...].astype(f32) + dot(chosen, w_back_ref[...])
    atom_out_ref[...] = jnp.where(iota((CAP, 1), 0) < count, back, 0.0).astype(bf16)


def attend_part(count, queries, kvs, bias, gate, state, mid, token, w_tok_out, w_back):
    return pl.pallas_call(
        attend_kernel,
        out_shape=[
            jax.ShapeDtypeStruct((TOK_DEV, C_TOK), bf16),
            jax.ShapeDtypeStruct((CAP, C_ATOM), bf16),
        ],
        in_specs=[SMEM] + [VMEM] * 9,
        out_specs=[VMEM] * 2,
        scratch_shapes=[
            pltpu.VMEM((COLS, TOK_DEV, MESSAGE), bf16),
            pltpu.VMEM((COLS, TOK_DEV, MESSAGE), bf16),
            pltpu.SemaphoreType.DMA((COLS,)),
            pltpu.SemaphoreType.DMA((COLS,)),
        ],
        compiler_params=pltpu.CompilerParams(
            collective_id=1, has_side_effects=True, vmem_limit_bytes=32 << 20
        ),
        name="attend_part",
    )(count, queries, kvs, bias, gate, state, mid, token, w_tok_out, w_back)


def local(
    atom_feat,
    atom_token,
    atom_count,
    window_start,
    w_atom_qkv,
    w_atom_out,
    w_atom_tok,
    single,
    tok_gain,
    w_tok,
    w_tok_out,
    pair,
    w_pair_in,
    w_pair_out,
    w_bias,
    w_back,
):
    tail = lax.dynamic_slice_in_dim(atom_feat, atom_count[0] - BEFORE, BEFORE, 0)
    prev_tail = shifted(tail, ("row", "col"), 1)
    next_head = shifted(atom_feat[:AFTER], ("row", "col"), -1)
    token = atom_token.reshape(1, CAP)
    mid, state, query, kv, gate = atom_part(
        atom_count, window_start, atom_feat, prev_tail, next_head, token, w_atom_qkv, w_atom_out,
        w_atom_tok, single, tok_gain.reshape(1, C_TOK), w_tok,
    )
    queries, kvs = exchange(query, kv)
    pair_out, bias = pair_part(pair, w_pair_in, w_pair_out, w_bias)
    token_out, atom_out = attend_part(
        atom_count, queries, kvs, bias, gate, state, mid, token, w_tok_out, w_back
    )
    return (token_out, atom_out, pair_out)


def solution(mesh):
    tokens = P(("row", "col"), None)
    flat = P(("row", "col"))
    return jax.shard_map(
        local,
        mesh=mesh,
        in_specs=(
            tokens, flat, flat, flat, P(), P(), P(), tokens, P(), P(), P(), P("row", "col", None),
            P(), P(), P(), P(),
        ),
        out_specs=(tokens, tokens, P("row", "col", None)),
        check_vma=False,
    )
```

time: 293 us -> 77.6 us (0.26)
  waiting for transfers between devices: 84.4 us -> 0.01 us
  other arithmetic: 74.9 us -> 0.01 us
  Pallas kernels: 0 us -> 62.7 us
  local copies, waits for them, and re-layouts: 58.4 us -> 6.16 us
  matrix products: 44.8 us -> 0 us
  between operations: 15.2 us -> 1.5 us
  starting transfers between devices: 13.2 us -> 6.83 us
    all_gather x1 -> x0, waiting for transfers between devices: 66.9 us -> none  [local(): lax.all_gather(projected[:, tok_width:3 * tok_width], ('row', 'col'), axi...]
    pallas_call x0 -> x4, Pallas kernels: none -> 62.7 us  [the longest x1 21.3 us: pair_part(): pl.pallas_call(pair_kernel, out_shape=[jax.ShapeDtypeStruct(pair.shape, b...]
    dot_general x35 -> x0, matrix products: 44.8 us -> none  [the longest x8 11.7 us: pair_piece(): jnp.einsum('kh,pk->hp', w_bias, renormed, preferred_element_type=jnp.floa...]
    reduce_sum x28 -> x0, other arithmetic: 43.2 us -> none  [the longest x17 29.1 us: layer_norm(): spread = jnp.mean(centred * centred, axis=-1, keepdims=True)]
    convert_element_type x16 -> x0, other arithmetic: 30.1 us -> none  [the longest x8 18.4 us: pair_piece(): normed = layer_norm(flat_tile.astype(jnp.float32)).astype(jnp.bfloat16)]
    gather x48 -> x0, local copies, waits for them, and re-layouts: 25.7 us -> none
    all_to_all x1 -> x0, waiting for transfers between devices: 17.5 us -> none  [local(): lax.all_to_all(pair_bias, 'col', split_axis=1, concat_axis=2, tiled=True)]
    slice x9 -> x1, local copies, waits for them, and re-layouts: 18.2 us -> 0.89 us  [local(): next_head = shifted(atom_feat[:AFTER], ('row', 'col'), -1)]
  transfers between devices with their start and end apart: 4 -> 2, of which waited for: 2 -> 0; matrix products, arithmetic and copies ran while one was open for 45% -> 3% of each run, Pallas kernels for 0% -> 28%
where the time goes in v1:
time: 77.6 us; the launch traced here: 77.2 us
  Pallas kernels  62.7 us (81%)
  starting transfers between devices  6.83 us (9%)
  local copies, waits for them, and re-layouts  6.16 us (8%)
  between operations  1.5 us (2%)
    pallas_call x1, Pallas kernels, pair_part(): pl.pallas_call(pair_kernel, out_shape=[jax.ShapeDtypeStruct(pair.shape, b...  21.3 us
    pallas_call x1, Pallas kernels, exchange(): pl.pallas_call(exchange_kernel, out_shape=[jax.ShapeDtypeStruct((COLS, TO...  19.6 us
    pallas_call x1, Pallas kernels, attend_part(): pl.pallas_call(attend_kernel, out_shape=[jax.ShapeDtypeStruct((TOK_DEV, C...  18.3 us
    ppermute x2, starting transfers between devices, shifted(): return lax.ppermute(block, axis, route)  6.83 us
    unnamed x29, local copies, waits for them, and re-layouts  3.84 us
    pallas_call x1, Pallas kernels, atom_part(): pl.pallas_call(atom_kernel, out_shape=[jax.ShapeDtypeStruct((CAP, C_ATOM)...  3.47 us
  transfers between devices with their start and end apart: 2, of which 0 were waited for; matrix products, arithmetic and copies ran while one was open for 3% of the time, Pallas kernels for 28%

profile of v1, /device:TPU:1, one launch (start us, length us, event | category | flops | bytes accessed | tf_op | source)
XLA Modules:
  0.0 77.2 jit_solution(17419725849778856117)
XLA Ops:
  0.6 0.0 copy-start.3
  0.6 0.0 slice-start
  0.7 0.0 copy-start.1
  0.7 0.0 copy-start.2
  0.7 0.0 copy-start
  0.7 0.9 %slice.3 = bf16[96,128]{1,0:T(8,128)(2,1)S(1)} slice(bf16[256,128]{1,0:T(8,128)(2,1)} %feat_ref.1), slice={[0:96], [0:128]} | slice | bytes 49152 | tf_op jit(solution)/shard_map/slice | solution.py:489
  1.6 3.3 %collective-permute-start.1 = (bf16[96,128]{1,0:T(8,128)(2,1)S(1)}, bf16[96,128]{1,0:T(8,128)(2,1)S(1)}, u32[]{:S(2)}, u32[]{:S(2)}) collective-permute-start(bf16[96,128]{1,0:T(8,128)(2,1)S(1)} %slice.3), channel_id=1, source_target_pairs={{1,0},{2,1},{3,2},{4,3},{5,4},{6,5},{7,6},{8,7},{9,8},{10,9},{11,1... | collective-permute-start | bytes 73736 | tf_op jit(solution)/shard_map/ppermute | solution.py:53
  5.6 0.7 constant_dynamic-slice_fusion
  6.3 3.5 %collective-permute-start = (bf16[64,128]{1,0:T(8,128)(2,1)S(1)}, bf16[64,128]{1,0:T(8,128)(2,1)S(1)}, u32[]{:S(2)}, u32[]{:S(2)}) collective-permute-start(bf16[64,128]{1,0:T(8,128)(2,1)S(1)} %constant_dynamic-slice_fusion), channel_id=1, source_target_pairs={{0,1},{1,2},{2,3},{3,4},{4,5},{5,6},{6,7},{7,8},{8,9},{9,10},{10,1... | collective-permute-start | bytes 49160 | tf_op jit(solution)/shard_map/ppermute | solution.py:53
  9.8 0.7 reshape.17.gain_ref
  10.5 0.8 %copy.19.w_bias_ref = bf16[128,16]{1,0:T(8,128)(2,1)S(1)} copy(bf16[128,16]{0,1:T(8,128)(2,1)} %param.30) | data formatting | bytes 8192 | tf_op args[14]
  11.3 0.0 copy-start.4
  11.3 0.9 %copy-done.4 = bf16[128,512]{1,0:T(8,128)(2,1)S(1)} copy-done((bf16[128,512]{1,0:T(8,128)(2,1)S(1)}, bf16[128,512]{1,0:T(8,128)(2,1)}, u32[]{:S(2)}) %copy-start.4) | copy-done | bytes 131096
  12.2 0.0 copy-start.6
  12.2 0.8 %copy-done.6 = bf16[256,128]{1,0:T(8,128)(2,1)S(1)} copy-done((bf16[256,128]{1,0:T(8,128)(2,1)S(1)}, bf16[256,128]{1,0:T(8,128)(2,1)}, u32[]{:S(2)}) %copy-start.6) | copy-done | bytes 65560
  13.1 0.0 slice-start.1
  13.1 0.0 copy-start.5
  13.1 0.0 copy-start.7
  13.1 0.0 copy-start.8
  13.1 0.0 copy-start.9
  13.1 0.0 copy-start.10
  13.1 21.3 %pair_part.1 = (bf16[256,128,128]{2,1,0:T(8,128)(2,1)}, bf16[256,16,128]{2,1,0:T(8,128)(2,1)S(1)}) custom-call(bf16[256,128,128]{2,1,0:T(8,128)(2,1)} %pair_ref.1, bf16[128,512]{1,0:T(8,128)(2,1)S(1)} %copy-done.4, bf16[256,128]{1,0:T(8,128)(2,1)S(1)} %copy-done.6, bf16[128,16]{1,0:T(8,128)(2,1)S(1)} %copy.19.w_bias_ref), custom_call_target="tpu_custom_call" | custom-call | tf_op jit(solution)/shard_map/pair_part/pallas_call | solution.py:313
  34.4 0.0 collective-permute-done.tail_ref
  34.4 0.0 collective-permute-done.1.head_ref
  34.4 0.0 copy-done.3
  34.4 0.0 slice-done
  34.4 0.0 copy-done.1
  34.4 0.0 slice-done.1
  34.4 0.0 copy-done.5
  34.4 0.0 copy-done.7
  34.5 0.0 copy-done.8
  34.5 0.0 copy-done.9
  34.5 0.0 copy-done.10
  34.5 3.5 %atom_part.1 = (bf16[256,128]{1,0:T(8,128)(2,1)S(1)}, f32[16,768]{1,0:T(8,128)S(1)}, bf16[16,768]{1,0:T(8,128)(2,1)S(1)}, bf16[16,1536]{1,0:T(8,128)(2,1)S(1)}, bf16[16,768]{1,0:T(8,128)(2,1)S(1)}) custom-call(s32[1]{0:T(128)S(6)} %copy.22.count_ref, s32[8]{0:T(128)S(1)} %copy-done.10, bf16[256,128]{1,0:T(8,128)(2,1)S(1)} %copy-done.3, ...), custom_call_target="tpu_custom_call" | custom-call | tf_op jit(solution)/shard_map/atom_part/pallas_call | solution.py:114
  38.0 19.6 %exchange.1 = (bf16[16,16,768]{2,1,0:T(8,128)(2,1)S(1)}, bf16[8,16,1536]{2,1,0:T(8,128)(2,1)S(1)}) custom-call(bf16[16,768]{1,0:T(8,128)(2,1)S(1)} %get-tuple-element.14.query_ref, bf16[16,1536]{1,0:T(8,128)(2,1)S(1)} %get-tuple-element.15.kv_ref), custom_call_target="tpu_custom_call" | custom-call | tf_op jit(solution)/shard_map/exchange/pallas_call | solution.py:228
  57.6 0.0 copy-done.2
  57.6 0.0 copy-done
  57.6 18.3 %attend_part.1 = (bf16[16,768]{1,0:T(8,128)(2,1)S(1)}, bf16[256,128]{1,0:T(8,128)(2,1)S(1)}) custom-call(s32[1]{0:T(128)S(6)} %copy.22.count_ref, bf16[16,16,768]{2,1,0:T(8,128)(2,1)S(1)} %get-tuple-element.16.queries_ref, bf16[8,16,1536]{2,1,0:T(8,128)(2,1)S(1)} %get-tuple-element.17.kvs_ref, bf16[256,16,128]{2,1,0:T(8,128)(2,1)S(1)} %get-tuple-element.18.bias_ref, ...), custom_call_target="tpu_custom_call" | custom-call | tf_op jit(solution)/shard_map/attend_part/pallas_call | solution.py:448
  75.9 0.6 copy.23
  76.5 0.6 copy.24
  (1 shorter events, 0.0 us)
Async XLA Ops:
  0.6 33.8 %copy-start.3 = (bf16[256,128]{1,0:T(8,128)(2,1)S(1)}, bf16[256,128]{1,0:T(8,128)(2,1)}, u32[]{:S(2)}) copy-start(bf16[256,128]{1,0:T(8,128)(2,1)} %feat_ref.1) | copy-start | bytes 196612
  0.6 33.8 %slice-start = ((s8[4718592]{0:T(1024)(128)(4,1)}), s8[524288]{0:T(1024)(128)(4,1)S(1)}, s32[]{:S(2)}) async-start(s8[4718592]{0:T(1024)(128)(4,1)} %bitcast.3), calls=%async_computation | async-start | bytes 1048576
  0.7 33.8 %copy-start.1 = (bf16[128,768]{1,0:T(8,128)(2,1)S(1)}, bf16[128,768]{1,0:T(8,128)(2,1)}, u32[]{:S(2)}) copy-start(bf16[128,768]{1,0:T(8,128)(2,1)} %w_lift_ref.1) | copy-start | bytes 589828
  0.7 56.9 %copy-start.2 = (bf16[768,128]{1,0:T(8,128)(2,1)S(1)}, bf16[768,128]{1,0:T(8,128)(2,1)}, u32[]{:S(2)}) copy-start(bf16[768,128]{1,0:T(8,128)(2,1)} %w_back_ref.1) | copy-start | bytes 589828
  0.7 56.9 %copy-start = (bf16[768,768]{1,0:T(8,128)(2,1)S(1)}, bf16[768,768]{1,0:T(8,128)(2,1)}, u32[]{:S(2)}) copy-start(bf16[768,768]{1,0:T(8,128)(2,1)} %w_tok_out_ref.1) | copy-start | bytes 3538948
  1.6 32.8 %collective-permute-start.1 = (bf16[96,128]{1,0:T(8,128)(2,1)S(1)}, bf16[96,128]{1,0:T(8,128)(2,1)S(1)}, u32[]{:S(2)}, u32[]{:S(2)}) collective-permute-start(bf16[96,128]{1,0:T(8,128)(2,1)S(1)} %slice.3), channel_id=1, source_target_pairs={{1,0},{2,1},{3,2},{4,3},{5,4},{6,5},{7,6},{8,7},{9,8},{10,9},{11,1... | collective-permute-start | bytes 73736 | tf_op jit(solution)/shard_map/ppermute | solution.py:53
  6.3 28.1 %collective-permute-start = (bf16[64,128]{1,0:T(8,128)(2,1)S(1)}, bf16[64,128]{1,0:T(8,128)(2,1)S(1)}, u32[]{:S(2)}, u32[]{:S(2)}) collective-permute-start(bf16[64,128]{1,0:T(8,128)(2,1)S(1)} %constant_dynamic-slice_fusion), channel_id=1, source_target_pairs={{0,1},{1,2},{2,3},{3,4},{4,5},{5,6},{6,7},{7,8},{8,9},{9,10},{10,1... | collective-permute-start | bytes 49160 | tf_op jit(solution)/shard_map/ppermute | solution.py:53
  11.3 0.9 %copy-start.4 = (bf16[128,512]{1,0:T(8,128)(2,1)S(1)}, bf16[128,512]{1,0:T(8,128)(2,1)}, u32[]{:S(2)}) copy-start(bf16[128,512]{1,0:T(8,128)(2,1)} %w_in_ref.1) | copy-start | bytes 393220
  12.2 0.8 %copy-start.6 = (bf16[256,128]{1,0:T(8,128)(2,1)S(1)}, bf16[256,128]{1,0:T(8,128)(2,1)}, u32[]{:S(2)}) copy-start(bf16[256,128]{1,0:T(8,128)(2,1)} %w_out_ref.3) | copy-start | bytes 196612
  13.1 21.4 %slice-start.1 = ((s8[4718592]{0:T(1024)(128)(4,1)}), s8[4194304]{0:T(1024)(128)(4,1)S(1)}, s32[]{:S(2)}) async-start(s8[4718592]{0:T(1024)(128)(4,1)} %bitcast.3), calls=%async_computation.1 | async-start | bytes 8388608
  13.1 21.4 %copy-start.5 = (bf16[128,384]{1,0:T(8,128)(2,1)S(1)}, bf16[128,384]{1,0:T(8,128)(2,1)}, u32[]{:S(2)}) copy-start(bf16[128,384]{1,0:T(8,128)(2,1)} %w_qkv_ref.1) | copy-start | bytes 294916
  13.1 21.4 %copy-start.7 = (bf16[128,128]{1,0:T(8,128)(2,1)S(1)}, bf16[128,128]{1,0:T(8,128)(2,1)}, u32[]{:S(2)}) copy-start(bf16[128,128]{1,0:T(8,128)(2,1)} %w_out_ref.2) | copy-start | bytes 98308
  13.1 21.4 %copy-start.8 = (bf16[16,768]{1,0:T(8,128)(2,1)S(1)}, bf16[16,768]{1,0:T(8,128)(2,1)}, u32[]{:S(2)}) copy-start(bf16[16,768]{1,0:T(8,128)(2,1)} %single_ref.1) | copy-start | bytes 73732
  13.1 21.4 %copy-start.9 = (s32[256]{0:T(256)S(1)}, s32[256]{0:T(256)}, u32[]{:S(2)}) copy-start(s32[256]{0:T(256)} %param.17) | copy-start | bytes 3076
  13.1 21.4 %copy-start.10 = (s32[8]{0:T(128)S(1)}, s32[8]{0:T(128)}, u32[]{:S(2)}) copy-start(s32[8]{0:T(128)} %starts_ref.1) | copy-start | bytes 100

commit v2 on v1

v2 whole, which is shorter than its diff:
```python
import functools
import math

import jax
import jax.numpy as jnp
from jax import lax
from jax.experimental import pallas as pl
from jax.experimental.pallas import tpu as pltpu
from jax.sharding import PartitionSpec as P

ATOM_HEADS = 4
TOK_HEADS = 16
QUERY_BLOCK = 32
KEY_WINDOW = 128
BEFORE = KEY_WINDOW // 2
AFTER = KEY_WINDOW - QUERY_BLOCK
CAP = 256
TOK_DEV = 16
C_ATOM = 128
C_TOK = 768
C_PAIR = 128
HID = 256
ROWS = 8
COLS = 16
TILE_I = 256
TILE_J = 128
MESSAGE = C_TOK + 128
EPS = 1e-05

f32 = jnp.float32
bf16 = jnp.bfloat16
MESH = pl.DeviceIdType.MESH
VMEM = pl.BlockSpec(memory_space=pltpu.VMEM)
SMEM = pl.BlockSpec(memory_space=pltpu.SMEM)
ANY = pl.BlockSpec(memory_space=pl.ANY)
HBM = pl.BlockSpec(memory_space=pltpu.HBM)


def dot(a, b):
    return jnp.dot(a, b, preferred_element_type=f32)


def dot_nt(a, b):
    return lax.dot_general(a, b, (((1,), (1,)), ((), ())), preferred_element_type=f32)


def iota(shape, dim):
    return lax.broadcasted_iota(jnp.int32, shape, dim)


def membership(token, live_count, block):
    shape = (TOK_DEV, CAP)
    local = token - block * TOK_DEV
    return ((iota(shape, 0) == local) & (iota(shape, 1) < live_count)).astype(f32)


CHUNK = 32
CHUNKS = TILE_I // CHUNK
EARLY = 1
BEFORE_ATTEND = 5
WINDOWS = (0, 128, 384, 512)
WIDE = 256
GROUP = 4


def atom_attention(block, count, starts_ref, feat, tail, head, w_qkv_ref, w_out_ref):
    last = ROWS * COLS - 1
    rows = jnp.concatenate([tail, feat, head], axis=0)
    length = rows.shape[0]
    queries = dot(feat, w_qkv_ref[:, :C_ATOM]).astype(bf16)
    keys_values = dot(rows, w_qkv_ref[:, C_ATOM:]).astype(bf16)
    keys, values = keys_values[:, :C_ATOM], keys_values[:, C_ATOM:]
    index = iota((1, length), 1)
    absent = -(1 << 20)
    shift_tail = jnp.where(block > 0, 0, absent)
    shift_head = jnp.where(block < last, count - CAP, absent)
    shift_own = jnp.where(index < BEFORE + count, 0, absent)
    position = index + jnp.where(
        index < BEFORE, shift_tail, jnp.where(index < BEFORE + CAP, shift_own, shift_head)
    )
    window = iota((CAP, 1), 0) // QUERY_BLOCK
    start = jnp.zeros((CAP, 1), jnp.int32)
    for b in range(CAP // QUERY_BLOCK):
        start = jnp.where(window == b, starts_ref[b] + BEFORE, start)
    allowed = (position >= start) & (position < start + KEY_WINDOW)
    width = C_ATOM // ATOM_HEADS
    lane = iota((CAP, C_ATOM), 1)
    mixed = jnp.zeros((CAP, C_ATOM), f32)
    for h in range(ATOM_HEADS):
        mine = (lane >= h * width) & (lane < (h + 1) * width)
        scores = dot_nt(jnp.where(mine, queries, jnp.zeros_like(queries)), keys)
        scores = jnp.where(allowed, scores * (1.0 / math.sqrt(width)), -1e30)
        weights = jnp.exp(scores - jnp.max(scores, axis=1, keepdims=True))
        total = jnp.sum(weights, axis=1, keepdims=True)
        mixed = jnp.where(mine, dot(weights.astype(bf16), values) / total, mixed)
    return (feat.astype(f32) + dot(mixed.astype(bf16), w_out_ref[...])).astype(bf16)


def main_kernel(
    count_ref, starts_hbm, feat_hbm, token_hbm, w_qkv_hbm, w_out_hbm, w_lift_hbm, single_hbm, gain_hbm, w_tok_hbm,
    pair_hbm, w_in_hbm, w_pair_out_hbm, w_bias_hbm,
    done, inbox, mid_ref, state_ref, gate_ref,
    starts_ref, feat_ref, token_ref, w_qkv_ref, w_out_ref, w_lift_ref, single_ref, gain_ref, w_tok_ref, w_in_ref, w_pair_out_ref,
    w_bias_ref, load_sem, held, pair_sem, w_up, w_down, bias_ref, tail_out, tail_ref, head_ref, halo_send, halo_recv,
    query_ref, kv_ref, queries_ref, kvs_ref, q_send, q_recv, kv_send, kv_recv, outbox, out_send, out_recv,
):
    r, c = lax.axis_index("row"), lax.axis_index("col")
    block = r * COLS + c
    last = ROWS * COLS - 1
    count = count_ref[0]
    sides = [
        (feat_hbm, feat_ref), (w_in_hbm, w_in_ref), (w_pair_out_hbm, w_pair_out_ref), (w_bias_hbm, w_bias_ref),
        (w_qkv_hbm, w_qkv_ref), (w_out_hbm, w_out_ref), (w_lift_hbm, w_lift_ref), (token_hbm, token_ref),
        (single_hbm, single_ref), (starts_hbm, starts_ref), (gain_hbm, gain_ref), (w_tok_hbm, w_tok_ref),
    ]
    loads = [
        pltpu.make_async_copy(src, dst, load_sem.at[n]) for n, (src, dst) in enumerate(sides)
    ]

    def chunk_at(t):
        return lax.rem(c // 2 + 1 + t, CHUNKS)

    def pair_load(t):
        k = chunk_at(t)
        rows = pl.ds(k * CHUNK, CHUNK)
        return pltpu.make_async_copy(pair_hbm.at[rows], held.at[rows], pair_sem.at[k])

    for load in loads[:4]:
        load.start()
    pair_load(0).start()
    for load in loads[4:]:
        load.start()
    for t in range(1, CHUNKS):
        pair_load(t).start()

    barrier = pltpu.get_barrier_semaphore()

    def greet(row, col):
        pl.semaphore_signal(barrier, inc=1, device_id=(row, col), device_id_type=MESH)

    def beside(distance):
        other = block + distance
        return other // COLS, lax.rem(other, COLS)

    def kv_source(k):
        return c // 2, lax.rem(c, 2) * ROWS + k

    def kv_target(k):
        return k, 2 * r + c // ROWS

    kv_here = c == 2 * r + c // ROWS

    def elsewhere(device):
        return (device[0] != r) | (device[1] != c)

    @pl.when(block > 0)
    def _():
        greet(*beside(-1))

    @pl.when(block < last)
    def _():
        greet(*beside(1))

    for k in range(1, COLS):
        greet(r, lax.rem(c + k, COLS))
    for k in range(ROWS):

        @pl.when(elsewhere(kv_source(k)))
        def _():
            greet(*kv_source(k))

    heard = (block > 0).astype(jnp.int32) + (block < last).astype(jnp.int32)
    pl.semaphore_wait(barrier, COLS - 1 + ROWS - kv_here.astype(jnp.int32) + heard)

    loads[0].wait()
    pick = iota((BEFORE, CAP), 1) == iota((BEFORE, CAP), 0) + (count - BEFORE)
    tail_out[...] = dot(pick.astype(bf16), feat_ref[...]).astype(bf16)

    def halo_copy(n, src, dst, distance):
        return pltpu.make_async_remote_copy(
            src_ref=src,
            dst_ref=dst,
            send_sem=halo_send.at[n],
            recv_sem=halo_recv.at[n],
            device_id=beside(distance),
            device_id_type=MESH,
        )

    def tail_copy():
        return halo_copy(0, tail_out, tail_ref, 1)

    def head_copy():
        return halo_copy(1, feat_ref.at[pl.ds(0, AFTER)], head_ref, -1)

    @pl.when(block < last)
    def _():
        tail_copy().start()

    @pl.when(block > 0)
    def _():
        head_copy().start()

    @pl.when(block == 0)
    def _():
        tail_ref[...] = jnp.zeros_like(tail_ref)

    @pl.when(block == last)
    def _():
        head_ref[...] = jnp.zeros_like(head_ref)

    for load in loads[1:4]:
        load.wait()
    w_in = w_in_ref[...].astype(f32)
    w_up[:HID] = (w_in[:, :HID].T * 0.5).astype(bf16)
    w_up[HID : 2 * HID] = w_in[:, HID:].T.astype(bf16)
    w_up[2 * HID :] = w_bias_ref[...]
    w_down[:C_PAIR] = w_pair_out_ref[...].astype(f32).T.astype(bf16)
    w_down[C_PAIR:] = dot_nt(w_bias_ref[...], w_pair_out_ref[...]).astype(bf16)
    bias_sum = jnp.sum(w_bias_ref[...].astype(f32), axis=1, keepdims=True)
    share = 1.0 / C_PAIR

    def pair_step(t):
        pair_load(t).wait()
        k = chunk_at(t)
        rows = pl.ds(k * CHUNK, CHUNK)
        tile = held[rows].reshape(CHUNK * TILE_J, C_PAIR).T
        wide = tile.astype(f32)
        mean = jnp.sum(wide, axis=0, keepdims=True) * share
        centred = wide - mean
        spread = jnp.sum(centred * centred, axis=0, keepdims=True) * share + EPS
        scale = lax.rsqrt(spread)
        up = dot(w_up[...], (centred * scale).astype(bf16))
        gate, value = up[:HID].astype(bf16), up[HID : 2 * HID].astype(bf16)
        hidden = (gate + gate * jnp.tanh(gate)) * value
        down = dot(w_down[...], hidden)
        updated = (wide + down[:C_PAIR]).astype(bf16)
        done[rows] = updated.T.reshape(CHUNK, TILE_J, C_PAIR)
        again = updated.astype(f32)
        mean_again = jnp.sum(again, axis=0, keepdims=True) * share
        centred = again - mean_again
        spread_again = jnp.sum(centred * centred, axis=0, keepdims=True) * share + EPS
        bias = up[2 * HID :] * (spread * scale) + down[C_PAIR:] + bias_sum * (mean - mean_again)
        bias = bias * lax.rsqrt(spread_again)
        for i in range(CHUNK):
            bias_ref[k, pl.ds(i, TOK_HEADS, stride=CHUNK), :] = bias[:, i * TILE_J : (i + 1) * TILE_J]

    def loop(first, stop, step):
        def body(t, carry):
            step(t)
            return carry

        lax.fori_loop(first, stop, body, 0)

    loop(0, EARLY, pair_step)

    @pl.when(block > 0)
    def _():
        halo_copy(0, tail_out, tail_ref, -1).wait_recv()
        head_copy().wait_send()

    @pl.when(block < last)
    def _():
        halo_copy(1, feat_ref.at[pl.ds(0, AFTER)], head_ref, 1).wait_recv()
        tail_copy().wait_send()

    for load in loads[4:]:
        load.wait()
    mid = atom_attention(
        block, count, starts_ref, feat_ref[...], tail_ref[...], head_ref[...], w_qkv_ref, w_out_ref
    )
    mid_ref[...] = mid
    lifted = jnp.maximum(dot(mid, w_lift_ref[...]), 0.0).astype(bf16)
    member = membership(token_ref[...], count, block)
    members = jnp.sum(member, axis=1, keepdims=True)
    state = single_ref[...].astype(f32) + dot(member.astype(bf16), lifted) / members
    state_ref[...] = state
    centred = state - jnp.mean(state, axis=1, keepdims=True)
    spread = jnp.mean(centred * centred, axis=1, keepdims=True)
    normed = (centred * lax.rsqrt(spread + EPS) * gain_ref[...].reshape(1, C_TOK)).astype(bf16)
    kv_ref[...] = dot(normed, w_tok_ref[:, C_TOK : 3 * C_TOK]).astype(bf16)

    def kv_copy(k):
        slot = lax.rem(c, ROWS)
        return pltpu.make_async_remote_copy(
            src_ref=kv_ref,
            dst_ref=kvs_ref.at[slot],
            send_sem=kv_send.at[k],
            recv_sem=kv_recv.at[slot],
            device_id=kv_target(k),
            device_id_type=MESH,
        )

    def kv_arrival(k):
        return pltpu.make_async_remote_copy(
            src_ref=kv_ref,
            dst_ref=kvs_ref.at[k],
            send_sem=kv_send.at[k],
            recv_sem=kv_recv.at[k],
            device_id=kv_source(k),
            device_id_type=MESH,
        )

    def q_copy(k):
        return pltpu.make_async_remote_copy(
            src_ref=query_ref,
            dst_ref=queries_ref.at[c],
            send_sem=q_send.at[k],
            recv_sem=q_recv.at[c],
            device_id=(r, lax.rem(c + k, COLS)),
            device_id_type=MESH,
        )

    def q_arrival(k):
        s = lax.rem(c + k, COLS)
        return pltpu.make_async_remote_copy(
            src_ref=query_ref,
            dst_ref=queries_ref.at[s],
            send_sem=q_send.at[k],
            recv_sem=q_recv.at[s],
            device_id=(r, s),
            device_id_type=MESH,
        )

    for k in range(ROWS):

        @pl.when(elsewhere(kv_target(k)))
        def _():
            kv_copy(k).start()

    query_ref[...] = dot(normed, w_tok_ref[:, :C_TOK]).astype(bf16)
    for k in range(1, COLS):
        q_copy(k).start()
    gate_ref[...] = dot(normed, w_tok_ref[:, 3 * C_TOK :]).astype(bf16)
    queries_ref[c] = query_ref[...]

    @pl.when(kv_here)
    def _():
        kvs_ref[lax.rem(c, ROWS)] = kv_ref[...]

    loop(EARLY, BEFORE_ATTEND, pair_step)

    for k in range(ROWS):

        @pl.when(elsewhere(kv_source(k)))
        def _():
            kv_arrival(k).wait_recv()

        @pl.when(elsewhere(kv_target(k)))
        def _():
            kv_copy(k).wait_send()

    for k in range(1, COLS):
        q_arrival(k).wait_recv()
        q_copy(k).wait_send()

    width = C_TOK // TOK_HEADS
    kvs = kvs_ref[...].reshape(TILE_J, 2 * C_TOK)
    column = iota((CHUNK, WIDE), 1)
    lane = iota((CHUNK, 128), 1)

    def out_copy(to):
        return pltpu.make_async_remote_copy(
            src_ref=outbox.at[to],
            dst_ref=inbox.at[c],
            send_sem=out_send.at[to],
            recv_sem=out_recv.at[c],
            device_id=(r, to),
            device_id_type=MESH,
        )

    def out_arrival(s):
        return pltpu.make_async_remote_copy(
            src_ref=outbox.at[s],
            dst_ref=inbox.at[s],
            send_sem=out_send.at[s],
            recv_sem=out_recv.at[s],
            device_id=(r, s),
            device_id_type=MESH,
        )

    def attend_step(t):
        k = chunk_at(t)
        pair_of = pl.ds(2 * k, 2)
        queries = queries_ref[pair_of].reshape(CHUNK, C_TOK)
        parts = []
        notes = jnp.zeros((CHUNK, 128), f32)
        for g, at in enumerate(WINDOWS):
            mine = [
                (column >= h * width - at) & (column < (h + 1) * width - at)
                for h in range(GROUP * g, GROUP * (g + 1))
            ]
            seen = queries[:, at : at + WIDE]
            stack = jnp.concatenate(
                [jnp.where(m, seen, jnp.zeros_like(seen)) for m in mine], axis=0
            )
            scores = dot_nt(stack, kvs[:, at : at + WIDE]) * (1.0 / math.sqrt(width))
            scores = scores + bias_ref[k, pl.ds(g * GROUP * CHUNK, GROUP * CHUNK), :]
            top = jnp.max(scores, axis=1, keepdims=True).astype(bf16).astype(f32)
            weights = jnp.exp(scores - top)
            total = jnp.sum(weights, axis=1, keepdims=True)
            mixed = dot(weights.astype(bf16), kvs[:, C_TOK + at : C_TOK + at + WIDE])
            part = jnp.zeros((CHUNK, WIDE), f32)
            for n, m in enumerate(mine):
                rows = slice(n * CHUNK, (n + 1) * CHUNK)
                part = jnp.where(m, mixed[rows], part)
                h = GROUP * g + n
                high = total[rows].astype(bf16).astype(f32)
                notes = jnp.where(lane == h, top[rows], notes)
                notes = jnp.where(lane == TOK_HEADS + h, high, notes)
                notes = jnp.where(lane == 2 * TOK_HEADS + h, total[rows] - high, notes)
            parts.append(part)
        half = WIDE // 2
        message = jnp.concatenate(
            [
                parts[0][:, :half], parts[0][:, half:] + parts[1][:, :half], parts[1][:, half:],
                parts[2][:, :half], parts[2][:, half:] + parts[3][:, :half], parts[3][:, half:], notes,
            ],
            axis=1,
        )
        outbox[pair_of] = message.astype(bf16).reshape(2, TOK_DEV, MESSAGE)
        for n in range(2):

            @pl.when(2 * k + n != c)
            def _():
                out_copy(2 * k + n).start()

    loop(0, BEFORE_ATTEND, attend_step)

    def both(t):
        pair_step(t)
        attend_step(t)

    loop(BEFORE_ATTEND, CHUNKS, both)
    inbox[c] = outbox[c]

    def arrived(k):
        s = lax.rem(c + k, COLS)
        out_arrival(s).wait_recv()
        out_copy(s).wait_send()

    loop(1, COLS, arrived)


def main_part(count, starts, feat, token, w_qkv, w_out, w_lift, single, gain, w_tok, pair, w_in, w_pair_out, w_bias):
    def vmem(*shape):
        return pltpu.VMEM(shape, bf16)

    def dma(n):
        return pltpu.SemaphoreType.DMA((n,))

    return pl.pallas_call(
        main_kernel,
        out_shape=[
            jax.ShapeDtypeStruct((TILE_I, TILE_J, C_PAIR), bf16),
            jax.ShapeDtypeStruct((COLS, TOK_DEV, MESSAGE), bf16),
            jax.ShapeDtypeStruct((CAP, C_ATOM), bf16),
            jax.ShapeDtypeStruct((TOK_DEV, C_TOK), f32),
            jax.ShapeDtypeStruct((TOK_DEV, C_TOK), bf16),
        ],
        in_specs=[SMEM] + [HBM] * 13,
        out_specs=[VMEM] * 5,
        scratch_shapes=[
            pltpu.SMEM((CAP // QUERY_BLOCK,), jnp.int32), vmem(CAP, C_ATOM), pltpu.VMEM((1, CAP), jnp.int32),
            vmem(C_ATOM, 3 * C_ATOM), vmem(C_ATOM, C_ATOM), vmem(C_ATOM, C_TOK), vmem(TOK_DEV, C_TOK),
            pltpu.VMEM((C_TOK,), f32), vmem(C_TOK, 4 * C_TOK), vmem(C_PAIR, 2 * HID), vmem(HID, C_PAIR),
            vmem(TOK_HEADS, C_PAIR), dma(12),
            vmem(TILE_I, TILE_J, C_PAIR), dma(CHUNKS),
            vmem(2 * HID + TOK_HEADS, C_PAIR), vmem(C_PAIR + TOK_HEADS, HID),
            pltpu.VMEM((CHUNKS, TOK_HEADS * CHUNK, TILE_J), f32),
            vmem(BEFORE, C_ATOM), vmem(BEFORE, C_ATOM), vmem(AFTER, C_ATOM), dma(2), dma(2),
            vmem(TOK_DEV, C_TOK), vmem(TOK_DEV, 2 * C_TOK),
            vmem(COLS, TOK_DEV, C_TOK), vmem(ROWS, TOK_DEV, 2 * C_TOK),
            dma(COLS), dma(COLS), dma(ROWS), dma(ROWS),
            vmem(COLS, TOK_DEV, MESSAGE), dma(COLS), dma(COLS),
        ],
        compiler_params=pltpu.CompilerParams(
            collective_id=0, has_side_effects=True, vmem_limit_bytes=36 << 20
        ),
        name="main_part",
    )(count, starts, feat, token, w_qkv, w_out, w_lift, single, gain, w_tok, pair, w_in, w_pair_out, w_bias)


def finish_kernel(
    count_ref, pair_ref, inbox, gate_ref, state_ref, mid_ref, token_ref, w_tok_out_ref, w_back_ref,
    token_out_ref, atom_out_ref, pair_out_ref, sem,
):
    write = pltpu.make_async_copy(pair_ref, pair_out_ref, sem)
    write.start()
    block = lax.axis_index("row") * COLS + lax.axis_index("col")
    width = C_TOK // TOK_HEADS
    head = iota((TOK_HEADS, C_TOK), 0) * width
    column = iota((TOK_HEADS, C_TOK), 1)
    head_one = ((column >= head) & (column < head + width)).astype(bf16)
    n = TOK_HEADS
    tails = [inbox[s, :, C_TOK:].astype(f32) for s in range(COLS)]
    tops = [t[:, :n] for t in tails]
    totals = [t[:, n : 2 * n] + t[:, 2 * n : 3 * n] for t in tails]
    top = functools.reduce(jnp.maximum, tops)
    factors = [jnp.exp(t - top) for t in tops]
    total = sum(f * t for f, t in zip(factors, totals))
    factors = jnp.concatenate([f / total for f in factors], axis=0)
    high = factors.astype(bf16)
    low = (factors - high.astype(f32)).astype(bf16)
    factors = dot(high, head_one) + dot(low, head_one)
    mixed = sum(
        factors[s * TOK_DEV : (s + 1) * TOK_DEV] * inbox[s, :, :C_TOK].astype(f32)
        for s in range(COLS)
    )
    gated = (mixed * jax.nn.sigmoid(gate_ref[...].astype(f32))).astype(bf16)
    token_out = (state_ref[...] + dot(gated, w_tok_out_ref[...])).astype(bf16)
    token_out_ref[...] = token_out
    count = count_ref[0]
    member = membership(token_ref[...], count, block).astype(bf16)
    same = (iota((CAP, CAP), 0) == iota((CAP, CAP), 1)).astype(bf16)
    chosen = dot(dot_nt(same, member).astype(bf16), token_out).astype(bf16)
    back = mid_ref[...].astype(f32) + dot(chosen, w_back_ref[...])
    atom_out_ref[...] = jnp.where(iota((CAP, 1), 0) < count, back, 0.0).astype(bf16)
    write.wait()


def finish_part(count, pair, inbox, gate, state, mid, token, w_tok_out, w_back):
    return pl.pallas_call(
        finish_kernel,
        out_shape=[
            jax.ShapeDtypeStruct((TOK_DEV, C_TOK), bf16),
            jax.ShapeDtypeStruct((CAP, C_ATOM), bf16),
            jax.ShapeDtypeStruct(pair.shape, bf16),
        ],
        in_specs=[SMEM, ANY] + [VMEM] * 7,
        out_specs=[VMEM, VMEM, ANY],
        scratch_shapes=[pltpu.SemaphoreType.DMA],
        compiler_params=pltpu.CompilerParams(vmem_limit_bytes=16 << 20),
        name="finish_part",
    )(count, pair, inbox, gate, state, mid, token, w_tok_out, w_back)


def local(
    atom_feat,
    atom_token,
    atom_count,
    window_start,
    w_atom_qkv,
    w_atom_out,
    w_atom_tok,
    single,
    tok_gain,
    w_tok,
    w_tok_out,
    pair,
    w_pair_in,
    w_pair_out,
    w_bias,
    w_back,
):
    token = atom_token.reshape(1, CAP)
    sides = (
        window_start, atom_feat, token, w_atom_qkv, w_atom_out, w_atom_tok, single, tok_gain, w_tok,
        pair, w_pair_in, w_pair_out, w_bias.T,
    )
    sides = [pltpu.with_memory_space_constraint(array, pltpu.HBM) for array in sides]
    pair_new, inbox, mid, state, gate = main_part(atom_count, *sides)
    return tuple(
        finish_part(atom_count, pair_new, inbox, gate, state, mid, token, w_tok_out, w_back)
    )


def solution(mesh):
    tokens = P(("row", "col"), None)
    flat = P(("row", "col"))
    return jax.shard_map(
        local,
        mesh=mesh,
        in_specs=(
            tokens, flat, flat, flat, P(), P(), P(), tokens, P(), P(), P(), P("row", "col", None),
            P(), P(), P(), P(),
        ),
        out_specs=(tokens, tokens, P("row", "col", None)),
        check_vma=False,
    )
```

time: 77.6 us -> 45.1 us (0.58)
  Pallas kernels: 62.7 us -> 43 us
  starting transfers between devices: 6.83 us -> 0 us
  local copies, waits for them, and re-layouts: 6.16 us -> 0.01 us
    pallas_call x4 -> x2, Pallas kernels: 62.7 us -> 43 us  [the longest x1 38.4 us: main_part(): pl.pallas_call(main_kernel, out_shape=[jax.ShapeDtypeStruct((TILE_I, TILE...]
    ppermute x2 -> x0, starting transfers between devices: 6.83 us -> none  [shifted(): return lax.ppermute(block, axis, route)]
    unnamed x29 -> x6, local copies, waits for them, and re-layouts: 3.84 us -> 0.01 us
    slice x1 -> x0, local copies, waits for them, and re-layouts: 0.89 us -> none  [local(): next_head = shifted(atom_feat[:AFTER], ('row', 'col'), -1)]
  transfers between devices with their start and end apart: 2 -> 0, of which waited for: 0 -> 0; matrix products, arithmetic and copies ran while one was open for 3% -> 0% of each run, Pallas kernels for 28% -> 0%
where the time goes in v2:
time: 45.1 us; the launch traced here: 44.7 us
  Pallas kernels  43 us (95%)
  between operations  1.6 us (4%)
    pallas_call x1, Pallas kernels, main_part(): pl.pallas_call(main_kernel, out_shape=[jax.ShapeDtypeStruct((TILE_I, TILE...  38.4 us
    pallas_call x1, Pallas kernels, finish_part(): pl.pallas_call(finish_kernel, out_shape=[jax.ShapeDtypeStruct((TOK_DEV, C...  4.65 us

profile of v2, /device:TPU:1, one launch (start us, length us, event | category | flops | bytes accessed | tf_op | source)
XLA Modules:
  0.0 44.7 jit_solution(4304392185899967197)
XLA Ops:
  0.6 0.0 copy-start.1
  0.6 0.0 copy-start
  0.7 0.0 copy-start.2
  1.4 38.4 %main_part.1 = (bf16[256,128,128]{2,1,0:T(8,128)(2,1)S(1)}, bf16[16,16,896]{2,1,0:T(8,128)(2,1)S(1)}, bf16[256,128]{1,0:T(8,128)(2,1)S(1)}, f32[16,768]{1,0:T(8,128)S(1)}, bf16[16,768]{1,0:T(8,128)(2,1)S(1)}) custom-call(s32[1]{0:T(128)S(6)} %copy.19.count_ref, s32[8]{0:T(128)} %starts_hbm.1, bf16[256,128]{1,0:T(8,128)(2,1)} %feat_hbm.1, s32[1,256]{1,0:T(1,128)} %bitcast.2, ...), custom_call_target="tpu_custom_call" | custom-call | tf_op jit(solution)/shard_map/main_part/pallas_call | solution.py:451
  39.8 0.0 copy-done.1
  39.8 0.0 copy-done
  39.8 0.0 copy-done.2
  39.9 4.6 %finish_part.1 = (bf16[16,768]{1,0:T(8,128)(2,1)}, bf16[256,128]{1,0:T(8,128)(2,1)}, bf16[256,128,128]{2,1,0:T(8,128)(2,1)}) custom-call(s32[1]{0:T(128)S(6)} %copy.19.count_ref, bf16[256,128,128]{2,1,0:T(8,128)(2,1)S(1)} %get-tuple-element.8.pair_ref, bf16[16,16,896]{2,1,0:T(8,128)(2,1)S(1)} %get-tuple-element.9.inbox, ...), custom_call_target="tpu_custom_call" | custom-call | tf_op jit(solution)/shard_map/finish_part/pallas_call | solution.py:522
Async XLA Ops:
  0.6 39.2 %copy-start.1 = (bf16[768,128]{1,0:T(8,128)(2,1)S(1)}, bf16[768,128]{1,0:T(8,128)(2,1)}, u32[]{:S(2)}) copy-start(bf16[768,128]{1,0:T(8,128)(2,1)} %w_back_ref.1) | copy-start | bytes 589828
  0.6 39.2 %copy-start = (bf16[768,768]{1,0:T(8,128)(2,1)S(1)}, bf16[768,768]{1,0:T(8,128)(2,1)}, u32[]{:S(2)}) copy-start(bf16[768,768]{1,0:T(8,128)(2,1)} %w_tok_out_ref.1) | copy-start | bytes 3538948
  0.7 39.2 %copy-start.2 = (s32[256]{0:T(256)S(1)}, s32[256]{0:T(256)}, u32[]{:S(2)}) copy-start(s32[256]{0:T(256)} %param.17) | copy-start | bytes 3076

commit v3 on v2

--- a/solution.py
+++ b/solution.py
@@ -57,7 +57,8 @@
 CHUNK = 32
 CHUNKS = TILE_I // CHUNK
 EARLY = 1
-BEFORE_ATTEND = 5
+PAIRED = 6
+SCHEDULE = ((0, 5), (1, 2), (1, 1))
 WINDOWS = (0, 128, 384, 512)
 WIDE = 256
 GROUP = 4
@@ -215,8 +216,12 @@
     w_up[HID : 2 * HID] = w_in[:, HID:].T.astype(bf16)
     w_up[2 * HID :] = w_bias_ref[...]
     w_down[:C_PAIR] = w_pair_out_ref[...].astype(f32).T.astype(bf16)
-    w_down[C_PAIR:] = dot_nt(w_bias_ref[...], w_pair_out_ref[...]).astype(bf16)
-    bias_sum = jnp.sum(w_bias_ref[...].astype(f32), axis=1, keepdims=True)
+    w_bias = w_bias_ref[...].astype(f32)
+    w_bias = w_bias - jnp.mean(w_bias, axis=1, keepdims=True)
+    high = w_bias.astype(bf16)
+    low = (w_bias - high.astype(f32)).astype(bf16)
+    w_pair_out = w_pair_out_ref[...]
+    w_down[C_PAIR:] = (dot_nt(high, w_pair_out) + dot_nt(low, w_pair_out)).astype(bf16)
     share = 1.0 / C_PAIR
 
     def pair_step(t):
@@ -233,18 +238,21 @@
         gate, value = up[:HID].astype(bf16), up[HID : 2 * HID].astype(bf16)
         hidden = (gate + gate * jnp.tanh(gate)) * value
         down = dot(w_down[...], hidden)
-        updated = (wide + down[:C_PAIR]).astype(bf16)
-        done[rows] = updated.T.reshape(CHUNK, TILE_J, C_PAIR)
-        again = updated.astype(f32)
-        mean_again = jnp.sum(again, axis=0, keepdims=True) * share
-        centred = again - mean_again
-        spread_again = jnp.sum(centred * centred, axis=0, keepdims=True) * share + EPS
-        bias = up[2 * HID :] * (spread * scale) + down[C_PAIR:] + bias_sum * (mean - mean_again)
+        moved = centred + down[:C_PAIR]
+        done[rows] = (moved + mean).astype(bf16).T.reshape(CHUNK, TILE_J, C_PAIR)
+        moved_mean = jnp.sum(moved, axis=0, keepdims=True) * share
+        spread_again = jnp.sum(moved * moved, axis=0, keepdims=True) * share
+        spread_again = jnp.maximum(spread_again - moved_mean * moved_mean, 0.0) + EPS
+        bias = up[2 * HID :] * (spread * scale) + down[C_PAIR:]
         bias = bias * lax.rsqrt(spread_again)
-        for i in range(CHUNK):
-            bias_ref[k, pl.ds(i, TOK_HEADS, stride=CHUNK), :] = bias[:, i * TILE_J : (i + 1) * TILE_J]
+        bias_ref[t] = bias.reshape(TOK_HEADS * CHUNK, TILE_J)
 
     def loop(first, stop, step):
+        if stop == first + 1:
+            step(first)
+        if stop <= first + 1:
+            return
+
         def body(t, carry):
             step(t)
             return carry
@@ -337,7 +345,7 @@
     def _():
         kvs_ref[lax.rem(c, ROWS)] = kv_ref[...]
 
-    loop(EARLY, BEFORE_ATTEND, pair_step)
+    loop(EARLY, PAIRED, pair_step)
 
     for k in range(ROWS):
 
@@ -378,59 +386,54 @@
             device_id_type=MESH,
         )
 
-    def attend_step(t):
-        k = chunk_at(t)
-        pair_of = pl.ds(2 * k, 2)
-        queries = queries_ref[pair_of].reshape(CHUNK, C_TOK)
-        parts = []
-        notes = jnp.zeros((CHUNK, 128), f32)
+    def attend(first, chunks):
+        places = [chunk_at(first + n) for n in range(chunks)]
+        queries = [queries_ref[pl.ds(2 * k, 2)].reshape(CHUNK, C_TOK) for k in places]
+        parts = [[] for _ in places]
+        notes = [jnp.zeros((CHUNK, 128), f32) for _ in places]
         for g, at in enumerate(WINDOWS):
-            mine = [
-                (column >= h * width - at) & (column < (h + 1) * width - at)
-                for h in range(GROUP * g, GROUP * (g + 1))
-            ]
-            seen = queries[:, at : at + WIDE]
-            stack = jnp.concatenate(
-                [jnp.where(m, seen, jnp.zeros_like(seen)) for m in mine], axis=0
-            )
-            scores = dot_nt(stack, kvs[:, at : at + WIDE]) * (1.0 / math.sqrt(width))
-            scores = scores + bias_ref[k, pl.ds(g * GROUP * CHUNK, GROUP * CHUNK), :]
+            heads = range(GROUP * g, GROUP * (g + 1))
+            mine = [(column >= h * width - at) & (column < (h + 1) * width - at) for h in heads]
+            stack = []
+            for q in queries:
+                seen = q[:, at : at + WIDE]
+                stack += [jnp.where(m, seen, jnp.zeros_like(seen)) for m in mine]
+            scores = dot_nt(jnp.concatenate(stack, axis=0), kvs[:, at : at + WIDE])
+            bias = bias_ref[pl.ds(first, chunks), pl.ds(g * GROUP * CHUNK, GROUP * CHUNK), :]
+            scores = scores * (1.0 / math.sqrt(width)) + bias.reshape(scores.shape)
             top = jnp.max(scores, axis=1, keepdims=True).astype(bf16).astype(f32)
             weights = jnp.exp(scores - top)
             total = jnp.sum(weights, axis=1, keepdims=True)
             mixed = dot(weights.astype(bf16), kvs[:, C_TOK + at : C_TOK + at + WIDE])
-            part = jnp.zeros((CHUNK, WIDE), f32)
-            for n, m in enumerate(mine):
-                rows = slice(n * CHUNK, (n + 1) * CHUNK)
-                part = jnp.where(m, mixed[rows], part)
-                h = GROUP * g + n
-                high = total[rows].astype(bf16).astype(f32)
-                notes = jnp.where(lane == h, top[rows], notes)
-                notes = jnp.where(lane == TOK_HEADS + h, high, notes)
-                notes = jnp.where(lane == 2 * TOK_HEADS + h, total[rows] - high, notes)
-            parts.append(part)
+            for n in range(chunks):
+                part = jnp.zeros((CHUNK, WIDE), f32)
+                for i, (h, m) in enumerate(zip(heads, mine)):
+                    rows = slice((n * GROUP + i) * CHUNK, (n * GROUP + i + 1) * CHUNK)
+                    part = jnp.where(m, mixed[rows], part)
+                    high = total[rows].astype(bf16).astype(f32)
+                    note = jnp.where(lane == h, top[rows], notes[n])
+                    note = jnp.where(lane == TOK_HEADS + h, high, note)
+                    notes[n] = jnp.where(lane == 2 * TOK_HEADS + h, total[rows] - high, note)
+                parts[n].append(part)
         half = WIDE // 2
-        message = jnp.concatenate(
-            [
-                parts[0][:, :half], parts[0][:, half:] + parts[1][:, :half], parts[1][:, half:],
-                parts[2][:, :half], parts[2][:, half:] + parts[3][:, :half], parts[3][:, half:], notes,
-            ],
-            axis=1,
-        )
-        outbox[pair_of] = message.astype(bf16).reshape(2, TOK_DEV, MESSAGE)
-        for n in range(2):
-
-            @pl.when(2 * k + n != c)
-            def _():
-                out_copy(2 * k + n).start()
-
-    loop(0, BEFORE_ATTEND, attend_step)
-
-    def both(t):
-        pair_step(t)
-        attend_step(t)
-
-    loop(BEFORE_ATTEND, CHUNKS, both)
+        for k, (a, b, d, e), note in zip(places, parts, notes):
+            message = [
+                a[:, :half], a[:, half:] + b[:, :half], b[:, half:],
+                d[:, :half], d[:, half:] + e[:, :half], e[:, half:], note,
+            ]
+            message = jnp.concatenate(message, axis=1).astype(bf16)
+            outbox[pl.ds(2 * k, 2)] = message.reshape(2, TOK_DEV, MESSAGE)
+            for n in range(2):
+
+                @pl.when(2 * k + n != c)
+                def _():
+                    out_copy(2 * k + n).start()
+
+    paired, attended = PAIRED, 0
+    for pairs, chunks in SCHEDULE:
+        loop(paired, paired + pairs, pair_step)
+        attend(attended, chunks)
+        paired, attended = paired + pairs, attended + chunks
     inbox[c] = outbox[c]
 
     def arrived(k):

time: 45.1 us -> 42.2 us (0.936)
  Pallas kernels: 43 us -> 40.4 us
    pallas_call x1, Pallas kernels: 38.4 us -> 35.8 us  [main_part(): pl.pallas_call(main_kernel, out_shape=[jax.ShapeDtypeStruct((TILE_I, TILE...]
where the time goes in v3:
time: 42.2 us; the launch traced here: 42.1 us
  Pallas kernels  40.4 us (96%)
  between operations  1.6 us (4%)
    pallas_call x1, Pallas kernels, main_part(): pl.pallas_call(main_kernel, out_shape=[jax.ShapeDtypeStruct((TILE_I, TILE...  35.8 us
    pallas_call x1, Pallas kernels, finish_part(): pl.pallas_call(finish_kernel, out_shape=[jax.ShapeDtypeStruct((TOK_DEV, C...  4.65 us

profile of v3, /device:TPU:1, one launch (start us, length us, event | category | flops | bytes accessed | tf_op | source)
XLA Modules:
  0.0 42.1 jit_solution(7021407030083328014)
XLA Ops:
  0.6 0.0 copy-start.1
  0.6 0.0 copy-start
  0.7 0.0 copy-start.2
  1.4 35.8 %main_part.1 = (bf16[256,128,128]{2,1,0:T(8,128)(2,1)S(1)}, bf16[16,16,896]{2,1,0:T(8,128)(2,1)S(1)}, bf16[256,128]{1,0:T(8,128)(2,1)S(1)}, f32[16,768]{1,0:T(8,128)S(1)}, bf16[16,768]{1,0:T(8,128)(2,1)S(1)}) custom-call(s32[1]{0:T(128)S(6)} %copy.19.count_ref, s32[8]{0:T(128)} %starts_hbm.1, bf16[256,128]{1,0:T(8,128)(2,1)} %feat_hbm.1, s32[1,256]{1,0:T(1,128)} %bitcast.2, ...), custom_call_target="tpu_custom_call" | custom-call | tf_op jit(solution)/shard_map/main_part/pallas_call | solution.py:454
  37.2 0.0 copy-done.1
  37.2 0.0 copy-done
  37.2 0.0 copy-done.2
  37.3 4.6 %finish_part.1 = (bf16[16,768]{1,0:T(8,128)(2,1)}, bf16[256,128]{1,0:T(8,128)(2,1)}, bf16[256,128,128]{2,1,0:T(8,128)(2,1)}) custom-call(s32[1]{0:T(128)S(6)} %copy.19.count_ref, bf16[256,128,128]{2,1,0:T(8,128)(2,1)S(1)} %get-tuple-element.8.pair_ref, bf16[16,16,896]{2,1,0:T(8,128)(2,1)S(1)} %get-tuple-element.9.inbox, ...), custom_call_target="tpu_custom_call" | custom-call | tf_op jit(solution)/shard_map/finish_part/pallas_call | solution.py:525
Async XLA Ops:
  0.6 36.6 %copy-start.1 = (bf16[768,128]{1,0:T(8,128)(2,1)S(1)}, bf16[768,128]{1,0:T(8,128)(2,1)}, u32[]{:S(2)}) copy-start(bf16[768,128]{1,0:T(8,128)(2,1)} %w_back_ref.1) | copy-start | bytes 589828
  0.6 36.6 %copy-start = (bf16[768,768]{1,0:T(8,128)(2,1)S(1)}, bf16[768,768]{1,0:T(8,128)(2,1)}, u32[]{:S(2)}) copy-start(bf16[768,768]{1,0:T(8,128)(2,1)} %w_tok_out_ref.1) | copy-start | bytes 3538948
  0.7 36.6 %copy-start.2 = (s32[256]{0:T(256)S(1)}, s32[256]{0:T(256)}, u32[]{:S(2)}) copy-start(s32[256]{0:T(256)} %param.17) | copy-start | bytes 3076

commit v4 on v3

--- a/solution.py
+++ b/solution.py
@@ -56,7 +56,7 @@
 
 CHUNK = 32
 CHUNKS = TILE_I // CHUNK
-EARLY = 1
+EARLY = 2
 PAIRED = 6
 SCHEDULE = ((0, 5), (1, 2), (1, 1))
 WINDOWS = (0, 128, 384, 512)
@@ -170,44 +170,9 @@
         def _():
             greet(*kv_source(k))
 
-    heard = (block > 0).astype(jnp.int32) + (block < last).astype(jnp.int32)
-    pl.semaphore_wait(barrier, COLS - 1 + ROWS - kv_here.astype(jnp.int32) + heard)
-
     loads[0].wait()
     pick = iota((BEFORE, CAP), 1) == iota((BEFORE, CAP), 0) + (count - BEFORE)
     tail_out[...] = dot(pick.astype(bf16), feat_ref[...]).astype(bf16)
-
-    def halo_copy(n, src, dst, distance):
-        return pltpu.make_async_remote_copy(
-            src_ref=src,
-            dst_ref=dst,
-            send_sem=halo_send.at[n],
-            recv_sem=halo_recv.at[n],
-            device_id=beside(distance),
-            device_id_type=MESH,
-        )
-
-    def tail_copy():
-        return halo_copy(0, tail_out, tail_ref, 1)
-
-    def head_copy():
-        return halo_copy(1, feat_ref.at[pl.ds(0, AFTER)], head_ref, -1)
-
-    @pl.when(block < last)
-    def _():
-        tail_copy().start()
-
-    @pl.when(block > 0)
-    def _():
-        head_copy().start()
-
-    @pl.when(block == 0)
-    def _():
-        tail_ref[...] = jnp.zeros_like(tail_ref)
-
-    @pl.when(block == last)
-    def _():
-        head_ref[...] = jnp.zeros_like(head_ref)
 
     for load in loads[1:4]:
         load.wait()
@@ -259,7 +224,43 @@
 
         lax.fori_loop(first, stop, body, 0)
 
-    loop(0, EARLY, pair_step)
+    loop(0, 1, pair_step)
+    heard = (block > 0).astype(jnp.int32) + (block < last).astype(jnp.int32)
+    pl.semaphore_wait(barrier, COLS - 1 + ROWS - kv_here.astype(jnp.int32) + heard)
+
+    def halo_copy(n, src, dst, distance):
+        return pltpu.make_async_remote_copy(
+            src_ref=src,
+            dst_ref=dst,
+            send_sem=halo_send.at[n],
+            recv_sem=halo_recv.at[n],
+            device_id=beside(distance),
+            device_id_type=MESH,
+        )
+
+    def tail_copy():
+        return halo_copy(0, tail_out, tail_ref, 1)
+
+    def head_copy():
+        return halo_copy(1, feat_ref.at[pl.ds(0, AFTER)], head_ref, -1)
+
+    @pl.when(block < last)
+    def _():
+        tail_copy().start()
+
+    @pl.when(block > 0)
+    def _():
+        head_copy().start()
+
+    @pl.when(block == 0)
+    def _():
+        tail_ref[...] = jnp.zeros_like(tail_ref)
+
+    @pl.when(block == last)
+    def _():
+        head_ref[...] = jnp.zeros_like(head_ref)
+
+    loop(1, EARLY, pair_step)
 
     @pl.when(block > 0)
     def _():

time: 42.2 us -> 41.1 us (0.974); the launches traced: 42.1 us -> 40.4 us
  Pallas kernels: 40.4 us -> 38.7 us
    pallas_call x1, Pallas kernels: 35.8 us -> 34.1 us  [main_part(): pl.pallas_call(main_kernel, out_shape=[jax.ShapeDtypeStruct((TILE_I, TILE...]
where the time goes in v4:
time: 41.1 us; the launch traced here: 40.4 us
  Pallas kernels  38.7 us (94%)
  between operations  1.6 us (4%)
    pallas_call x1, Pallas kernels, main_part(): pl.pallas_call(main_kernel, out_shape=[jax.ShapeDtypeStruct((TILE_I, TILE...  34.1 us
    pallas_call x1, Pallas kernels, finish_part(): pl.pallas_call(finish_kernel, out_shape=[jax.ShapeDtypeStruct((TOK_DEV, C...  4.65 us

profile of v4, /device:TPU:1, one launch (start us, length us, event | category | flops | bytes accessed | tf_op | source)
XLA Modules:
  0.0 40.4 jit_solution(12004700509745915772)
XLA Ops:
  0.6 0.0 copy-start.1
  0.6 0.0 copy-start
  0.7 0.0 copy-start.2
  1.4 34.1 %main_part.1 = (bf16[256,128,128]{2,1,0:T(8,128)(2,1)S(1)}, bf16[16,16,896]{2,1,0:T(8,128)(2,1)S(1)}, bf16[256,128]{1,0:T(8,128)(2,1)S(1)}, f32[16,768]{1,0:T(8,128)S(1)}, bf16[16,768]{1,0:T(8,128)(2,1)S(1)}) custom-call(s32[1]{0:T(128)S(6)} %copy.19.count_ref, s32[8]{0:T(128)} %starts_hbm.1, bf16[256,128]{1,0:T(8,128)(2,1)} %feat_hbm.1, s32[1,256]{1,0:T(1,128)} %bitcast.2, ...), custom_call_target="tpu_custom_call" | custom-call | tf_op jit(solution)/shard_map/main_part/pallas_call | solution.py:455
  35.5 0.0 copy-done.1
  35.5 0.0 copy-done
  35.5 0.0 copy-done.2
  35.5 4.6 %finish_part.1 = (bf16[16,768]{1,0:T(8,128)(2,1)}, bf16[256,128]{1,0:T(8,128)(2,1)}, bf16[256,128,128]{2,1,0:T(8,128)(2,1)}) custom-call(s32[1]{0:T(128)S(6)} %copy.19.count_ref, bf16[256,128,128]{2,1,0:T(8,128)(2,1)S(1)} %get-tuple-element.8.pair_ref, bf16[16,16,896]{2,1,0:T(8,128)(2,1)S(1)} %get-tuple-element.9.inbox, ...), custom_call_target="tpu_custom_call" | custom-call | tf_op jit(solution)/shard_map/finish_part/pallas_call | solution.py:526
Async XLA Ops:
  0.6 34.9 %copy-start.1 = (bf16[768,128]{1,0:T(8,128)(2,1)S(1)}, bf16[768,128]{1,0:T(8,128)(2,1)}, u32[]{:S(2)}) copy-start(bf16[768,128]{1,0:T(8,128)(2,1)} %w_back_ref.1) | copy-start | bytes 589828
  0.6 34.9 %copy-start = (bf16[768,768]{1,0:T(8,128)(2,1)S(1)}, bf16[768,768]{1,0:T(8,128)(2,1)}, u32[]{:S(2)}) copy-start(bf16[768,768]{1,0:T(8,128)(2,1)} %w_tok_out_ref.1) | copy-start | bytes 3538948
  0.7 34.9 %copy-start.2 = (s32[256]{0:T(256)S(1)}, s32[256]{0:T(256)}, u32[]{:S(2)}) copy-start(s32[256]{0:T(256)} %param.17) | copy-start | bytes 3076
